TPU v7x, 32 devices: a whole 2x2x4 slice. The times are simulated.
32 devices in a mesh: batch: 8 (over z, core), tensor: 4 (over y, x).
Axes of the slice: x: 2, y: 2, z: 4, core: 2. Of those that a mesh axis runs over, the one named last changes fastest.
Arguments:
- tokens: bfloat16 [12288, 1024], P(('batch', 'tensor')), may hold values from -60 to 60
- output_grad: bfloat16 [12288, 1024], P(('batch', 'tensor')), may hold values from -6 to 6
- attn_norm_gain: bfloat16 [1024], replicated, may hold values from 0.099609375 to 1.8984375
- attn_norm_bias: bfloat16 [1024], replicated, may hold values from -3 to 3
- mlp_norm_gain: bfloat16 [1024], replicated, may hold values from 0.099609375 to 1.8984375
- mlp_norm_bias: bfloat16 [1024], replicated, may hold values from -3 to 3
- qkv_weight: bfloat16 [1024, 3072], P(None, 'tensor'), may hold values from -0.1875 to 0.1875
- qkv_bias: bfloat16 [3072], P('tensor'), may hold values from -3 to 3
- dense_weight: bfloat16 [1024, 1024], P('tensor'), may hold values from -0.75 to 0.75
- dense_bias: bfloat16 [1024], replicated, may hold values from -3 to 3
- fc_weight: bfloat16 [1024, 4096], P(None, 'tensor'), may hold values from -0.1875 to 0.1875
- fc_bias: bfloat16 [4096], P('tensor'), may hold values from -3 to 3
- proj_weight: bfloat16 [4096, 1024], P('tensor'), may hold values from -0.09375 to 0.09375
- feature_weight: bfloat16 [16, 64, 64], P('tensor'), may hold values from -0.75 to 0.75
- seq_units: int32 [8, 4], P('batch'), may hold values from 1 to 6, 12 in all within a row
- pad_tokens: int32 [8, 4], P('batch'), may hold values from 0 to 63
Outputs:
- output: bfloat16 [12288, 1024], P(('batch', 'tensor'))
- tokens_grad: bfloat16 [12288, 1024], P(('batch', 'tensor'))
- attn_norm_gain_grad: float32 [1024], replicated
- attn_norm_bias_grad: float32 [1024], replicated
- mlp_norm_gain_grad: float32 [1024], replicated
- mlp_norm_bias_grad: float32 [1024], replicated
- qkv_weight_grad: float32 [1024, 3072], P(None, 'tensor')
- qkv_bias_grad: float32 [3072], P('tensor')
- dense_weight_grad: float32 [1024, 1024], P('tensor')
- dense_bias_grad: float32 [1024], replicated
- fc_weight_grad: float32 [1024, 4096], P(None, 'tensor')
- fc_bias_grad: float32 [4096], P('tensor')
- proj_weight_grad: float32 [4096, 1024], P('tensor')
- feature_weight_grad: float32 [16, 64, 64], P('tensor')
Inputs may be any that keep to these rules, and one draw needn't show every extreme that they name: `seq_units`: the lengths of a group's 4 sequences add up to 12 units.
All inputs are finite; a program needn't handle non-finite values.
Results may differ from a plain program's by a relative error of at most 0.011.
Values may be sent and summed in bfloat16 or wider, within the bound.
No kernel may reach another device: no remote copies, remote signals or barrier semaphores. Data moves between devices by JAX's collectives and lax.ppermute only.
A program may use at most 192 MiB of HBM per device.

v0:
```python
from functools import partial
import math

import jax
import jax.numpy as jnp
from jax import lax
from jax.sharding import PartitionSpec as P

ROT = 16
SPAN = 64
UNIT = 128


highest = lax.Precision.HIGHEST
epsilon = 1e-05


def cosine_table(dimension):
    spatial = jnp.arange(dimension, dtype=jnp.float32)[:, None]
    frequency = jnp.arange(dimension, dtype=jnp.float32)[None, :]
    dct_table = jnp.cos(
        math.pi * (2.0 * spatial + 1.0) * frequency / (2.0 * dimension)
    ) * math.sqrt(2.0 / dimension)
    return jnp.where(frequency == 0.0, dct_table * math.sqrt(0.5), dct_table)


def rotate(values, cosines, sines, direction):
    half_rot = cosines.shape[-1]
    leading = values[..., :half_rot]
    trailing = values[..., half_rot : 2 * half_rot]
    return jnp.concatenate(
        [
            leading * cosines - direction * trailing * sines,
            trailing * cosines + direction * leading * sines,
            values[..., 2 * half_rot :],
        ],
        axis=-1,
    )


def rotary_angles(position):
    half_rot = ROT // 2
    inverse_freq = jnp.exp(-math.log(10000.0) * 2.0 * jnp.arange(half_rot, dtype=jnp.float32) / ROT)
    angles = position.astype(jnp.float32)[:, None] * inverse_freq[None, :]
    return (jnp.cos(angles)[:, None, :], jnp.sin(angles)[:, None, :])


def group_layout(unit_counts, pad_counts, group_rows):
    seq_ends = jnp.cumsum(unit_counts) * UNIT
    starts = seq_ends - unit_counts * UNIT
    row_ids = jnp.arange(group_rows, dtype=jnp.int32)
    member = (row_ids[:, None] >= starts[None, :]) & (row_ids[:, None] < seq_ends[None, :])
    first_row = jnp.sum(jnp.where(member, starts[None, :], 0), axis=1)
    last_real = jnp.sum(jnp.where(member, (seq_ends - pad_counts)[None, :], 0), axis=1)
    span_member = member[::SPAN].astype(jnp.float32)
    same_seq = jnp.dot(span_member, span_member.T)
    span_ids = jnp.arange(span_member.shape[0], dtype=jnp.int32)
    before = jnp.where(span_ids[:, None] > span_ids[None, :], same_seq, 0.0)
    return (row_ids - first_row, (row_ids < last_real).astype(jnp.float32), before)


def body(
    tokens,
    output_grad,
    attn_norm_gain,
    attn_norm_bias,
    mlp_norm_gain,
    mlp_norm_bias,
    qkv_weight,
    qkv_bias,
    dense_weight,
    dense_bias,
    fc_weight,
    fc_bias,
    proj_weight,
    feature_weight,
    seq_units,
    pad_tokens,
):
    rows_dev, width = tokens.shape
    parts = lax.axis_size("tensor")
    group_rows = rows_dev * parts
    heads_local, head_dim, num_feat = feature_weight.shape
    spans = group_rows // SPAN
    qkv_cols = qkv_weight.shape[1]
    x_float = tokens.astype(jnp.float32)
    row_mean = jnp.mean(x_float, axis=-1, keepdims=True)
    centered = x_float - row_mean
    inv_std = lax.rsqrt(jnp.mean(centered * centered, axis=-1, keepdims=True) + epsilon)
    x_hat = centered * inv_std
    gain_one = attn_norm_gain.astype(jnp.float32)
    gain_two = mlp_norm_gain.astype(jnp.float32)
    normed_one = (x_hat * gain_one + attn_norm_bias.astype(jnp.float32)).astype(jnp.bfloat16)
    normed_two = (x_hat * gain_two + mlp_norm_bias.astype(jnp.float32)).astype(jnp.bfloat16)
    rows_one, rows_two = (
        lax.all_gather(normed_one, "tensor", axis=0, tiled=True),
        lax.all_gather(normed_two, "tensor", axis=0, tiled=True),
    )
    position, is_real, before = group_layout(seq_units[0], pad_tokens[0], group_rows)
    cosines, sines = rotary_angles(position)
    dct_table = cosine_table(head_dim)
    feat_weight = feature_weight.astype(jnp.float32)
    packed = jnp.dot(rows_one, qkv_weight, preferred_element_type=jnp.float32) + qkv_bias.astype(
        jnp.float32
    )
    packed = packed.reshape(group_rows, heads_local, 3, head_dim)
    query = packed[:, :, 0]
    key_rows = packed[:, :, 1]
    value_rows = packed[:, :, 2].astype(jnp.bfloat16)

    def spectrum_of(head_rows):
        spectrum = jnp.einsum(
            "ghd,de->ghe", rotate(head_rows, cosines, sines, 1.0), dct_table, precision=highest
        )
        return (
            spectrum,
            jnp.exp(jnp.einsum("ghd,hdm->ghm", spectrum, feat_weight, precision=highest)),
        )

    spectrum_q, exp_query = spectrum_of(query)
    spectrum_k, exp_key = spectrum_of(key_rows)
    exp_key = exp_key * is_real[:, None, None]
    span_query = exp_query.astype(jnp.bfloat16).reshape(spans, SPAN, heads_local, num_feat)
    span_key = exp_key.astype(jnp.bfloat16).reshape(spans, SPAN, heads_local, num_feat)
    span_value = value_rows.reshape(spans, SPAN, heads_local, head_dim)
    causal = jnp.tril(jnp.ones((SPAN, SPAN), jnp.float32))
    scores = (
        jnp.einsum("cthm,cshm->chts", span_query, span_key, preferred_element_type=jnp.float32)
        * causal
    )
    state = jnp.einsum("cshm,cshd->chmd", span_key, span_value, preferred_element_type=jnp.float32)
    key_total = jnp.sum(span_key, axis=1, dtype=jnp.float32)
    prior = jnp.einsum("ce,ehmd->chmd", before, state, precision=highest)
    prior_total = jnp.einsum("ce,ehm->chm", before, key_total, precision=highest)
    numer = jnp.einsum("chts,cshd->cthd", scores, span_value, precision=highest) + jnp.einsum(
        "cthm,chmd->cthd", span_query, prior, precision=highest
    )
    denom = jnp.transpose(jnp.sum(scores, axis=3), (0, 2, 1)) + jnp.einsum(
        "cthm,chm->cth", span_query, prior_total, precision=highest
    )
    attended = numer / denom[..., None]
    mixed = attended.reshape(group_rows, heads_local * head_dim).astype(jnp.bfloat16)
    hidden = jnp.dot(rows_two, fc_weight, preferred_element_type=jnp.float32) + fc_bias.astype(
        jnp.float32
    )
    gelu_exact = partial(jax.nn.gelu, approximate=False)
    activated_wide, gelu_back = jax.vjp(gelu_exact, hidden)
    activated = activated_wide.astype(jnp.bfloat16)
    part_act = lax.slice_in_dim(activated, 0, rows_dev * lax.axis_size("tensor"), axis=0)
    branch_total = lax.psum_scatter(
        jnp.dot(mixed, dense_weight, preferred_element_type=jnp.float32)
        + jnp.dot(part_act, proj_weight, preferred_element_type=jnp.float32),
        "tensor",
        scatter_dimension=0,
        tiled=True,
    )
    output = (x_float + branch_total + dense_bias.astype(jnp.float32)).astype(jnp.bfloat16)
    grad_all = lax.all_gather(output_grad, "tensor", axis=0, tiled=True)
    grad_mixed = jnp.einsum(
        "gd,ad->ga", grad_all, dense_weight, preferred_element_type=jnp.float32
    ).astype(jnp.bfloat16)
    dense_grad = jnp.einsum("ga,gd->ad", mixed, grad_all, preferred_element_type=jnp.float32)
    proj_grad = jnp.einsum("gf,gd->fd", activated, grad_all, preferred_element_type=jnp.float32)
    grad_act = jnp.einsum("gd,fd->gf", grad_all, proj_weight, preferred_element_type=jnp.float32)
    grad_hidden = gelu_back(grad_act)[0].astype(jnp.bfloat16)
    fc_grad = jnp.einsum("ge,gf->ef", rows_two, grad_hidden, preferred_element_type=jnp.float32)
    fc_bias_grad = jnp.sum(grad_hidden, axis=0, dtype=jnp.float32)
    grad_out = grad_mixed.astype(jnp.float32).reshape(spans, SPAN, heads_local, head_dim)
    grad_numer = grad_out / denom[..., None]
    grad_denom = -jnp.sum(grad_out * attended, axis=-1) / denom
    grad_scores = (
        jnp.einsum("cthd,cshd->chts", grad_numer, span_value, precision=highest)
        + jnp.transpose(grad_denom, (0, 2, 1))[..., None]
    ) * causal
    later = jnp.einsum("cthm,cthd->chmd", span_query, grad_numer, precision=highest)
    later_total = jnp.einsum("cthm,cth->chm", span_query, grad_denom, precision=highest)
    after = jnp.einsum("ec,ehmd->chmd", before, later, precision=highest)
    after_total = jnp.einsum("ec,ehm->chm", before, later_total, precision=highest)
    grad_qfeat = (
        jnp.einsum("chts,cshm->cthm", grad_scores, span_key, precision=highest)
        + jnp.einsum("cthd,chmd->cthm", grad_numer, prior, precision=highest)
        + grad_denom[..., None] * prior_total[:, None]
    )
    grad_kfeat = (
        jnp.einsum("chts,cthm->cshm", grad_scores, span_query, precision=highest)
        + jnp.einsum("cshd,chmd->cshm", span_value, after, precision=highest)
        + after_total[:, None]
    )
    grad_value = jnp.einsum("chts,cthd->cshd", scores, grad_numer, precision=highest) + jnp.einsum(
        "cshm,chmd->cshd", span_key, after, precision=highest
    )
    logit_grad_q = grad_qfeat.reshape(group_rows, heads_local, num_feat) * exp_query
    logit_grad_k = grad_kfeat.reshape(group_rows, heads_local, num_feat) * exp_key
    feature_grad = jnp.einsum(
        "ghd,ghm->hdm", spectrum_q, logit_grad_q, precision=highest
    ) + jnp.einsum("ghd,ghm->hdm", spectrum_k, logit_grad_k, precision=highest)

    def unturn(logit_grad):
        grad_spectrum = jnp.einsum("ghm,hdm->ghd", logit_grad, feat_weight, precision=highest)
        grad_turned = jnp.einsum("ghe,de->ghd", grad_spectrum, dct_table, precision=highest)
        return rotate(grad_turned, cosines, sines, -1.0)

    grad_qkv = jnp.stack(
        [
            unturn(logit_grad_q),
            unturn(logit_grad_k),
            grad_value.reshape(group_rows, heads_local, head_dim),
        ],
        axis=2,
    )
    grad_qkv = grad_qkv.reshape(group_rows, qkv_cols).astype(jnp.bfloat16)
    qkv_grad = jnp.einsum("ge,gc->ec", rows_one, grad_qkv, preferred_element_type=jnp.float32)
    qkv_bias_grad = jnp.sum(grad_qkv, axis=0, dtype=jnp.float32)
    both_norms = lax.psum_scatter(
        jnp.concatenate(
            [
                jnp.einsum("gc,ec->ge", grad_qkv, qkv_weight, preferred_element_type=jnp.float32),
                jnp.einsum("gf,ef->ge", grad_hidden, fc_weight, preferred_element_type=jnp.float32),
            ],
            axis=1,
        ),
        "tensor",
        scatter_dimension=0,
        tiled=True,
    )
    norm_one_grad = both_norms[:, :width]
    norm_two_grad = both_norms[:, width:]
    grad_float = output_grad.astype(jnp.float32)
    grad_hat = norm_one_grad * gain_one + norm_two_grad * gain_two
    grad_input = inv_std * (
        grad_hat
        - jnp.mean(grad_hat, axis=-1, keepdims=True)
        - x_hat * jnp.mean(grad_hat * x_hat, axis=-1, keepdims=True)
    )
    tokens_grad = (grad_float + grad_input).astype(jnp.bfloat16)
    gain_one_grad, bias_one_grad, gain_two_grad, bias_two_grad, dense_bias_grad = lax.psum(
        (
            jnp.sum(norm_one_grad * x_hat, axis=0),
            jnp.sum(norm_one_grad, axis=0),
            jnp.sum(norm_two_grad * x_hat, axis=0),
            jnp.sum(norm_two_grad, axis=0),
            jnp.sum(grad_float, axis=0),
        ),
        ("batch", "tensor"),
    )
    qkv_grad, qkv_bias_grad, dense_grad, fc_grad, fc_bias_grad, proj_grad, feature_grad = lax.psum(
        (qkv_grad, qkv_bias_grad, dense_grad, fc_grad, fc_bias_grad, proj_grad, feature_grad),
        "batch",
    )
    return (
        output,
        tokens_grad,
        gain_one_grad,
        bias_one_grad,
        gain_two_grad,
        bias_two_grad,
        qkv_grad,
        qkv_bias_grad,
        dense_grad,
        dense_bias_grad,
        fc_grad,
        fc_bias_grad,
        proj_grad,
        feature_grad,
    )


def solution(mesh):
    placed = (
        P(("batch", "tensor"), None),
        P(("batch", "tensor"), None),
        P(),
        P(),
        P(),
        P(),
        P(None, "tensor"),
        P("tensor"),
        P("tensor", None),
        P(),
        P(None, "tensor"),
        P("tensor"),
        P("tensor", None),
        P("tensor", None, None),
        P("batch", None),
        P("batch", None),
    )
    return jax.shard_map(
        body,
        mesh=mesh,
        in_specs=placed,
        out_specs=(
            P(("batch", "tensor"), None),
            P(("batch", "tensor"), None),
            P(),
            P(),
            P(),
            P(),
            P(None, "tensor"),
            P("tensor"),
            P("tensor", None),
            P(),
            P(None, "tensor"),
            P("tensor"),
            P("tensor", None),
            P("tensor", None, None),
        ),
        check_vma=False,
    )
```

profile of v0, /device:TPU:0, one launch (start us, length us, event | category | flops | bytes accessed | tf_op | source)
XLA Modules:
  0.0 743.2 jit_solution(17525988518465334594)
XLA Ops:
  19.1 43.6 %all-gather.4.cloned.1.call-done = bf16[1536,1024]{1,0:T(8,128)(2,1)} async-done(((bf16[384,1024]{1,0:T(8,128)(2,1)}), bf16[1536,1024]{1,0:T(8,128)(2,1)}) %all-gather.4.cloned.1.call-update) | async-done | bytes 3145744 | tf_op jit(solution)/shard_map/all_gather | solution.py:96
  62.6 5.1 convolution_add_fusion.1
  108.8 5.9 fusion.8
  124.5 5.0 copy.173
  129.6 6.1 fusion.142
  135.7 4.5 multiply_reduce_fusion
  145.5 5.9 fusion.6
  155.4 6.8 fusion.150
  165.1 4.8 bitcast_add_fusion
  177.2 6.3 add_bitcast_fusion.1
  204.4 5.6 add_bitcast_fusion
  219.0 4.6 fusion.152
  223.6 6.1 fusion.148
  229.8 19.1 %convert_reduce_fusion = (f32[1024]{0:T(1024)S(1)}, bf16[1536,1024]{1,0:T(8,128)(2,1)S(1)}, f32[1536,1024]{1,0:T(8,128)}) fusion(f32[1536,1024]{1,0:T(8,128)S(1)} %fusion.148, f32[1024]{0:T(1024)S(1)} %convert_element_type.115, bf16[1536,1024]{1,0:T(8,128)(2,1)S(1)} %copy-done.59, bf16[1024,1024]{1,0:T(8,128)(2,1)S(1)} %copy-done), kind=kOutput, calls=%fused_computation.3 | convolution fusion | flops 3339189248 | bytes 20979712 | tf_op jit(solution)/shard_map/gd,fd->gf/dot_general | solution.py:164
  250.6 5.8 fusion.153
  256.3 11.3 %pad_maximum_fusion = f32[1536,2048]{1,0:T(8,128)} fusion(f32[1536,1024]{1,0:T(8,128)} %fusion.153, f32[1536,1024]{1,0:T(8,128)} %fusion.152), kind=kLoop, calls=%fused_computation | loop fusion | flops 3145728 | bytes 25165824 | tf_op jit(solution)/shard_map/concatenate | solution.py:215
  273.9 6.9 multiply_convert_fusion
  301.1 5.0 fusion.157
  306.1 5.0 fusion.156
  311.9 17.7 %all-reduce.1 = (f32[768]{0:T(1024)}, f32[1024]{0:T(1024)}) all-reduce(f32[768]{0:T(1024)S(1)} %reduce_sum.160, f32[1024]{0:T(1024)S(1)} %get-tuple-element.36), channel_id=1, replica_groups=mesh['batch'=8,'tensor'=4] {'batch'}, use_global_device_ids=true, to_apply=%region_22.23 | all-reduce | flops 1792 | bytes 14336 | tf_op jit(solution)/shard_map/psum | solution.py:246
  329.6 58.8 %reduce-scatter.5.cloned.1.call-done = f32[384,2048]{1,0:T(8,128)} async-done(((f32[1536,2048]{1,0:T(8,128)}), f32[384,2048]{1,0:T(8,128)}) %reduce-scatter.5.cloned.1.call-update) | async-done | bytes 3145744 | tf_op jit(solution)/shard_map/reduce_scatter | solution.py:214
  392.4 69.1 %reduce-scatter.3.cloned.1.call-done = f32[384,1024]{1,0:T(8,128)} async-done(((f32[1536,1024]{1,0:T(8,128)}), f32[384,1024]{1,0:T(8,128)}) %reduce-scatter.3.cloned.1.call-update) | async-done | bytes 1572880 | tf_op jit(solution)/shard_map/reduce_scatter | solution.py:150
  465.5 41.0 %all-reduce = (f32[1024]{0:T(1024)}, f32[1024]{0:T(1024)}, f32[1024]{0:T(1024)}, f32[1024]{0:T(1024)}, f32[1024]{0:T(1024)}) all-reduce(f32[1024]{0:T(1024)S(1)} %get-tuple-element.18, f32[1024]{0:T(1024)S(1)} %get-tuple-element.17, f32[1024]{0:T(1024)S(1)} %get-tuple-element.19, ...), channel_id=1, replica_groups=mesh['batch'=8,'tensor'=4] {'batch','tensor'}, use_global_device_ids=true, to_apply=%region_13.14 | all-reduce | flops 5120 | bytes 40960 | tf_op jit(solution)/shard_map/psum | solution.py:236
  506.5 218.4 %all-reduce.5.cloned.1.call-done = (f32[1024,768]{1,0:T(8,128)}, f32[256,1024]{1,0:T(8,128)}, f32[1024,1024]{1,0:T(8,128)}, f32[1024,1024]{1,0:T(8,128)}, f32[4,64,64]{2,1,0:T(8,128)}) async-done(((f32[1024,768]{1,0:T(8,128)}, f32[256,1024]{1,0:T(8,128)}, f32[1024,1024]{1,0:T(8,128)}, f32[1024,1024]{1,0:T(8,128)}, f32[4,64,64]{2,1,0:T(8,128)}), (f32[1024,768]{1,0:T(8,128)}, f32[256,1024]{1,0:T(8,128)}, ...) | async-done | bytes 12648464 | tf_op jit(solution)/shard_map/psum | solution.py:246
  (243 shorter events, 159.5 us)
Async XLA Ops:
  7.2 222.6 %copy-start = (bf16[1024,1024]{1,0:T(8,128)(2,1)S(1)}, bf16[1024,1024]{1,0:T(8,128)(2,1)}, u32[]{:S(2)}) copy-start(bf16[1024,1024]{1,0:T(8,128)(2,1)} %param.28) | copy-start | bytes 6291460
  7.2 10.2 %copy-start.53 = (bf16[768]{0:T(1024)(128)(2,1)S(1)}, bf16[768]{0:T(1024)(128)(2,1)}, u32[]{:S(2)}) copy-start(bf16[768]{0:T(1024)(128)(2,1)} %param.23) | copy-start | bytes 4612
  7.2 10.2 %copy-start.56 = (s32[1,4]{1,0:T(1,128)S(1)}, s32[1,4]{1,0:T(1,128)}, u32[]{:S(2)}) copy-start(s32[1,4]{1,0:T(1,128)} %param.30) | copy-start | bytes 52
  7.2 10.4 %copy-start.57 = (s32[1,4]{1,0:T(1,128)S(1)}, s32[1,4]{1,0:T(1,128)}, u32[]{:S(2)}) copy-start(s32[1,4]{1,0:T(1,128)} %param.31) | copy-start | bytes 52
  7.2 10.9 %copy-start.54 = (bf16[1024]{0:T(1024)(128)(2,1)S(1)}, bf16[1024]{0:T(1024)(128)(2,1)}, u32[]{:S(2)}) copy-start(bf16[1024]{0:T(1024)(128)(2,1)} %param.27) | copy-start | bytes 6148
  7.2 55.4 %all-gather.4.cloned.1.call-start = ((), (), s32[]{:S(2)}) async-start(), calls=%async_computation.2 | async-start | bytes 3932160 | tf_op jit(solution)/shard_map/all_gather | solution.py:96
  15.8 100.6 %all-gather.8.cloned.1.call-start = ((), (), s32[]{:S(2)}) async-start(), calls=%async_computation.5 | async-start | bytes 3932160 | tf_op jit(solution)/shard_map/all_gather | solution.py:158
  16.6 207.1 %all-gather.6.cloned.1.call-start = ((), (), s32[]{:S(2)}) async-start(), calls=%async_computation.3 | async-start | bytes 3932160 | tf_op jit(solution)/shard_map/all_gather | solution.py:97
  17.3 371.2 %reduce-scatter.5.cloned.1.call-start = ((), (), s32[]{:S(2)}) async-start(), calls=%async_computation.6 | async-start | bytes 15728640 | tf_op jit(solution)/shard_map/reduce_scatter | solution.py:214
  17.4 159.8 %copy-start.38 = (f32[64,64]{0,1:T(8,128)}, f32[64,64]{0,1:T(8,128)S(1)}, u32[]{:S(2)}) copy-start(f32[64,64]{0,1:T(8,128)S(1)} %fusion.97) | copy-start | bytes 49156
  19.1 50.4 %copy-start.42 = (f32[1536,8]{0,1:T(8,128)}, f32[1536,8]{0,1:T(8,128)S(1)}, u32[]{:S(2)}) copy-start(f32[1536,8]{0,1:T(8,128)S(1)} %get-tuple-element.68) | copy-start | bytes 147460
  108.8 7.7 %copy-start.40 = (bf16[256,1024]{1,0:T(8,128)(2,1)S(1)}, bf16[256,1024]{1,0:T(8,128)(2,1)}, u32[]{:S(2)}) copy-start(bf16[256,1024]{1,0:T(8,128)(2,1)} %param.24) | copy-start | bytes 1572868
  155.4 6.9 copy-start.1
  155.4 6.9 copy-start.18
  229.8 19.1 %copy-start.19 = (f32[1536,1024]{1,0:T(8,128)}, f32[1536,1024]{1,0:T(8,128)S(1)}, u32[]{:S(2)}) copy-start(f32[1536,1024]{1,0:T(8,128)S(1)} %fusion.148) | copy-start | bytes 18874372
  229.8 20.8 %copy-start.62 = (bf16[1024,1024]{1,0:T(8,128)(2,1)S(1)}, bf16[1024,1024]{1,0:T(8,128)(2,1)}, u32[]{:S(2)}) copy-start(bf16[1024,1024]{1,0:T(8,128)(2,1)} %param.26) | copy-start | bytes 6291460
  267.7 193.9 %reduce-scatter.3.cloned.1.call-start = ((), (), s32[]{:S(2)}) async-start(), calls=%async_computation.4 | async-start | bytes 7864320 | tf_op jit(solution)/shard_map/reduce_scatter | solution.py:150
  288.1 436.8 %all-reduce.5.cloned.1.call-start = ((), (), s32[]{:S(2)}) async-start(), calls=%async_computation.7 | async-start | bytes 25427968 | tf_op jit(solution)/shard_map/psum | solution.py:246
  288.3 6.4 copy-start.60
  311.1 77.3 %copy-start.4 = (bf16[384,1024]{1,0:T(8,128)(2,1)S(1)}, bf16[384,1024]{1,0:T(8,128)(2,1)}, u32[]{:S(2)}) copy-start(bf16[384,1024]{1,0:T(8,128)(2,1)} %param.16) | copy-start | bytes 2359300
  311.1 77.3 %copy-start.46 = (f32[384]{0:T(512)S(1)}, f32[384]{0:T(512)}, u32[]{:S(2)}) copy-start(f32[384]{0:T(512)} %copy-done.45) | copy-start | bytes 4612
  311.1 77.3 %copy-start.48 = (f32[1024]{0:T(1024)S(1)}, f32[1024]{0:T(1024)}, u32[]{:S(2)}) copy-start(f32[1024]{0:T(1024)} %copy-done.47) | copy-start | bytes 12292
  311.1 77.3 %copy-start.50 = (f32[1024]{0:T(1024)S(1)}, f32[1024]{0:T(1024)}, u32[]{:S(2)}) copy-start(f32[1024]{0:T(1024)} %copy-done.49) | copy-start | bytes 12292
  311.2 77.3 %copy-start.52 = (f32[384]{0:T(512)S(1)}, f32[384]{0:T(512)}, u32[]{:S(2)}) copy-start(f32[384]{0:T(512)} %copy-done.51) | copy-start | bytes 4612
  (48 other events, 169.9 us)
Sparse Core Ops, SparseCore 0:
  15.9 46.6 all-gather.3
  64.5 43.9 all-gather.7
  110.9 43.9 all-gather.5
  267.8 120.6 reduce-scatter.4
  391.3 70.1 reduce-scatter.2
  465.3 259.5 all-reduce.4
where the time goes:
time: 751 us; the launch traced here: 743 us
  waiting for transfers between devices  391 us (52%)
  matrix products  157 us (21%)
  local copies, waits for them, and re-layouts  79.5 us (11%)
  blocking collectives  58.8 us (8%)
  other arithmetic  41 us (5%)
  between operations  15.2 us (2%)
    psum x1, waiting for transfers between devices, body(): lax.psum((qkv_grad, qkv_bias_grad, dense_grad, fc_grad, fc_bias_grad, pro...  218 us
    reduce_scatter x1, waiting for transfers between devices, body(): lax.psum_scatter(jnp.dot(mixed, dense_weight, preferred_element_type=jnp....  69.1 us
    reduce_scatter x1, waiting for transfers between devices, body(): lax.psum_scatter(jnp.concatenate([jnp.einsum('gc,ec->ge', grad_qkv, qkv_w...  58.8 us
    all_gather x1, waiting for transfers between devices, body(): lax.all_gather(normed_one, 'tensor', axis=0, tiled=True)  43.6 us
    psum x1, blocking collectives, body(): lax.psum((jnp.sum(norm_one_grad * x_hat, axis=0), jnp.sum(norm_one_grad,...  41 us
    unnamed x138, local copies, waits for them, and re-layouts  22.9 us
    dot_general x1, matrix products, body(): jnp.einsum('gd,fd->gf', grad_all, proj_weight, preferred_element_type=jnp...  19.1 us
    psum x1, blocking collectives, body(): lax.psum((qkv_grad, qkv_bias_grad, dense_grad, fc_grad, fc_bias_grad, pro...  17.7 us
  transfers between devices with their start and end apart: 6, of which 4 were waited for; matrix products, arithmetic and copies ran while one was open for 28% of the time, Pallas kernels for 0%

commit v1 on v0

v1 whole, which is shorter than its diff:
```python
from functools import partial
import math

import jax
import jax.numpy as jnp
from jax import lax
from jax.experimental import pallas as pl
from jax.experimental.pallas import tpu as pltpu
from jax.sharding import PartitionSpec as P

ROT = 16
UNIT = 128
EPS = 1e-05
F32 = jnp.float32
BF16 = jnp.bfloat16
VMEM_BYTES = 56 * 1024 * 1024

NN = (((1,), (0,)), ((), ()))
NT = (((1,), (1,)), ((), ()))
TN = (((0,), (0,)), ((), ()))


def mm(a, b, dims=NN):
    return lax.dot_general(a, b, dims, preferred_element_type=F32)


def split(a):
    hi = a.astype(BF16)
    return hi, (a - hi.astype(F32)).astype(BF16)


def params(grid_rank=1):
    return pltpu.CompilerParams(
        dimension_semantics=("arbitrary",) * grid_rank, vmem_limit_bytes=VMEM_BYTES
    )


def whole(shape):
    return pl.BlockSpec(shape, lambda *_: (0,) * len(shape))


def rows_of(block, width):
    return pl.BlockSpec((block, width), lambda i: (i, 0))


def norm_rows(x):
    mean = jnp.mean(x, axis=-1, keepdims=True)
    cent = x - mean
    inv = lax.rsqrt(jnp.mean(cent * cent, axis=-1, keepdims=True) + EPS)
    return cent * inv, inv


def fwd_kernel(x, vec, wqkv, bqkv, wfc, bfc, lna_o, lnm_o, qk_o, v_o, act_o, gp_o):
    xh, _ = norm_rows(x[...].astype(F32))
    lna = (xh * vec[0:1, :] + vec[1:2, :]).astype(BF16)
    lnm = (xh * vec[2:3, :] + vec[3:4, :]).astype(BF16)
    lna_o[...] = lna
    lnm_o[...] = lnm
    qkv = mm(lna, wqkv[...]) + bqkv[...]
    two = qk_o.shape[1]
    qk_o[...] = qkv[:, :two]
    v_o[...] = qkv[:, two:].astype(BF16)
    h = mm(lnm, wfc[...]) + bfc[...]
    cdf = 0.5 + 0.5 * lax.erf(h * math.sqrt(0.5))
    act_o[...] = (h * cdf).astype(BF16)
    gp_o[...] = (cdf + h * (jnp.exp(-0.5 * h * h) * (1.0 / math.sqrt(2.0 * math.pi)))).astype(BF16)


def fwd_call(x, vec, wqkv, bqkv, wfc, bfc):
    rows, width = x.shape
    cols, hid = wqkv.shape[1], wfc.shape[1]
    w = cols // 3
    rb = 256
    flops = 2 * rows * width * (cols + hid)
    return pl.pallas_call(
        fwd_kernel,
        grid=(rows // rb,),
        in_specs=[
            rows_of(rb, width),
            whole(vec.shape),
            whole(wqkv.shape),
            whole(bqkv.shape),
            whole(wfc.shape),
            whole(bfc.shape),
        ],
        out_specs=[
            rows_of(rb, width),
            rows_of(rb, width),
            rows_of(rb, 2 * w),
            rows_of(rb, w),
            rows_of(rb, hid),
            rows_of(rb, hid),
        ],
        out_shape=[
            jax.ShapeDtypeStruct((rows, width), BF16),
            jax.ShapeDtypeStruct((rows, width), BF16),
            jax.ShapeDtypeStruct((rows, 2 * w), F32),
            jax.ShapeDtypeStruct((rows, w), BF16),
            jax.ShapeDtypeStruct((rows, hid), BF16),
            jax.ShapeDtypeStruct((rows, hid), BF16),
        ],
        compiler_params=params(),
        cost_estimate=pl.CostEstimate(
            flops=flops, bytes_accessed=rows * width * 20, transcendentals=rows * hid
        ),
        name="norm_qkv_fc",
    )(x, vec, wqkv, bqkv, wfc, bfc)


def chunk_place(units, pads, chunk, nseq):
    start = jnp.int32(0)
    pos, real, last = jnp.int32(0), jnp.int32(0), jnp.int32(0)
    for n in range(nseq):
        u = units[0, n]
        inside = (chunk >= start) & (chunk < start + u)
        pos = jnp.where(inside, chunk - start, pos)
        real = jnp.where(inside, (start + u - chunk) * UNIT - pads[0, n], real)
        last = jnp.where(inside, (chunk == start + u - 1).astype(jnp.int32), last)
        start = start + u
    return pos, real, last


def lanes(table, w):
    return jnp.concatenate([table] * (w // table.shape[1]), axis=1) if w > table.shape[1] else table


def turn(a, cosines, sines, low_half):
    w = a.shape[1]
    other = jnp.where(low_half, pltpu.roll(a, w - ROT // 2, 1), pltpu.roll(a, ROT // 2, 1))
    return a * cosines + other * sines


def head_stack(a, head_of_lane, heads):
    zero = jnp.zeros_like(a)
    return jnp.concatenate([jnp.where(head_of_lane == h, a, zero) for h in range(heads)], axis=0)


def side_by_side(a, heads):
    return jnp.concatenate([a[h * UNIT : (h + 1) * UNIT, :] for h in range(heads)], axis=1)


def masks(w, hd):
    lane = lax.broadcasted_iota(jnp.int32, (UNIT, w), 1)
    head_of_lane = lane // hd
    low_half = (lane % hd) < ROT // 2
    bi = lax.broadcasted_iota(jnp.int32, (w, w), 0) // hd
    bj = lax.broadcasted_iota(jnp.int32, (w, w), 1) // hd
    heads = w // hd
    row = lax.broadcasted_iota(jnp.int32, (heads * UNIT, UNIT), 0) % UNIT
    col = lax.broadcasted_iota(jnp.int32, (heads * UNIT, UNIT), 1)
    return head_of_lane, low_half, bi == bj, row >= col


def attn_fwd_kernel(
    nseq, hd, per, units, pads, qk, v_ref, cf, cos_t, sin_t,
    ao_o, o_o, rd_o, fq_o, fk_o, rq_o, rk_o, s_o, ks_o, state, ksum,
):
    w = v_ref.shape[1]
    heads = w // hd
    step = pl.program_id(0)
    head_of_lane, low_half, diag, causal = masks(w, hd)
    ones_bd = jnp.where(diag, 1.0, 0.0).astype(BF16)
    head_ones = head_stack(jnp.ones((UNIT, w), BF16), head_of_lane, heads)
    cf_hi, cf_lo = cf[0], cf[1]

    @pl.when(step == 0)
    def _():
        state[...] = jnp.zeros_like(state)
        ksum[...] = jnp.zeros_like(ksum)

    row_id = lax.broadcasted_iota(jnp.int32, (UNIT, 1), 0)
    for i in range(per):
        pos, real, _ = chunk_place(units, pads, step * per + i, nseq)
        rows = pl.ds(i * UNIT, UNIT)
        at = pl.ds(pl.multiple_of(pos * UNIT, UNIT), UNIT)
        cosines = lanes(cos_t[at, :], w)
        sines = lanes(sin_t[at, :], w)
        keep = jnp.where(pos == 0, 0.0, 1.0)
        s_old = state[...] * keep
        k_old = ksum[...] * keep
        rq = turn(qk[rows, 0:w], cosines, sines, low_half)
        rk = turn(qk[rows, w : 2 * w], cosines, sines, low_half)
        rq_o[rows, :] = rq.astype(BF16)
        rk_o[rows, :] = rk.astype(BF16)
        qh, ql = split(rq)
        kh, kl = split(rk)
        fq = jnp.exp(mm(qh, cf_hi) + mm(ql, cf_hi) + mm(qh, cf_lo)).astype(BF16)
        ek = jnp.exp(mm(kh, cf_hi) + mm(kl, cf_hi) + mm(kh, cf_lo))
        fk = jnp.where(row_id < real, ek, 0.0).astype(BF16)
        fq_o[rows, :] = fq
        fk_o[rows, :] = fk
        v = v_ref[rows, :]
        s_hi, s_lo = split(s_old)
        s_o[i, 0] = s_hi
        s_o[i, 1] = s_lo
        ks_o[i] = k_old
        scores = jnp.where(causal, mm(head_stack(fq, head_of_lane, heads), fk, NT), 0.0).astype(BF16)
        wide = side_by_side(scores, heads)
        num = mm(wide, head_stack(v, head_of_lane, heads)) + mm(fq, s_hi) + mm(fq, s_lo)
        p_hi, p_lo = split(fq.astype(F32) * k_old)
        den = mm(wide, head_ones) + mm(p_hi, ones_bd) + mm(p_lo, ones_bd)
        rden = 1.0 / den
        o = num * rden
        o_o[rows, :] = o
        rd_o[rows, :] = rden
        ao_o[rows, :] = o.astype(BF16)
        state[...] = s_old + jnp.where(diag, mm(fk, v, TN), 0.0)
        ksum[...] = k_old + jnp.sum(fk.astype(F32), axis=0, keepdims=True)


def attn_fwd_call(units, pads, qk, v, cf, cos_t, sin_t, hd, parts):
    rows, w = v.shape
    block = rows // parts
    per = block // UNIT
    nseq = units.shape[1]
    n = rows // UNIT
    smem = pl.BlockSpec(memory_space=pltpu.SMEM)
    sds = jax.ShapeDtypeStruct
    return pl.pallas_call(
        partial(attn_fwd_kernel, nseq, hd, per),
        grid=(parts,),
        in_specs=[
            smem,
            smem,
            rows_of(block, 2 * w),
            rows_of(block, w),
            whole(cf.shape),
            whole(cos_t.shape),
            whole(sin_t.shape),
        ],
        out_specs=[rows_of(block, w)] * 7
        + [
            pl.BlockSpec((per, 2, w, w), lambda i: (i, 0, 0, 0)),
            pl.BlockSpec((per, 1, w), lambda i: (i, 0, 0)),
        ],
        out_shape=[
            sds((rows, w), BF16),
            sds((rows, w), F32),
            sds((rows, w), F32),
            sds((rows, w), BF16),
            sds((rows, w), BF16),
            sds((rows, w), BF16),
            sds((rows, w), BF16),
            sds((n, 2, w, w), BF16),
            sds((n, 1, w), F32),
        ],
        scratch_shapes=[pltpu.VMEM((w, w), F32), pltpu.VMEM((1, w), F32)],
        compiler_params=params(),
        cost_estimate=pl.CostEstimate(
            flops=6_000_000_000, bytes_accessed=rows * w * 24, transcendentals=2 * rows * w
        ),
        name="attn_fwd",
    )(units, pads, qk, v, cf, cos_t, sin_t)


def attn_bwd_kernel(
    nseq, hd, per, units, pads, dao, v_ref, o_ref, rd_ref, fq_ref, fk_ref, rq_ref, rk_ref, s_ref, ks_ref,
    cf, cos_t, sin_t, dqkv_o, g_o, sum_o, after, after_sum,
):
    w = v_ref.shape[1]
    heads = w // hd
    step = pl.program_id(0)
    block = pl.num_programs(0) - 1 - step
    head_of_lane, low_half, diag, causal = masks(w, hd)
    ones_bd = jnp.where(diag, 1.0, 0.0).astype(BF16)
    cf_hi, cf_lo = cf[0], cf[1]

    @pl.when(step == 0)
    def _():
        after[...] = jnp.zeros_like(after)
        after_sum[...] = jnp.zeros_like(after_sum)
        g_o[...] = jnp.zeros_like(g_o)
        sum_o[...] = jnp.zeros_like(sum_o)

    for i in reversed(range(per)):
        pos, _, last = chunk_place(units, pads, block * per + i, nseq)
        rows = pl.ds(i * UNIT, UNIT)
        at = pl.ds(pl.multiple_of(pos * UNIT, UNIT), UNIT)
        cosines = lanes(cos_t[at, :], w)
        sines = -lanes(sin_t[at, :], w)
        keep = jnp.where(last == 1, 0.0, 1.0)
        a_old = after[...] * keep
        as_old = after_sum[...] * keep
        fq, fk, v = fq_ref[rows, :], fk_ref[rows, :], v_ref[rows, :]
        fqf, fkf = fq.astype(F32), fk.astype(F32)
        dn = (dao[rows, :].astype(F32) * rd_ref[rows, :]).astype(BF16)
        p_hi, p_lo = split(dn.astype(F32) * o_ref[rows, :])
        dden = -(mm(p_hi, ones_bd) + mm(p_lo, ones_bd))
        dn_s = head_stack(dn, head_of_lane, heads)
        fq_s = head_stack(fq, head_of_lane, heads)
        dden_s = jnp.concatenate(
            [jnp.broadcast_to(dden[:, h * hd : h * hd + 1], (UNIT, UNIT)) for h in range(heads)], axis=0
        )
        da = jnp.where(causal, mm(dn_s, v, NT) + dden_s, 0.0).astype(BF16)
        a = jnp.where(causal, mm(fq_s, fk, NT), 0.0).astype(BF16)
        s_hi, s_lo = s_ref[i, 0], s_ref[i, 1]
        dfq = (
            mm(side_by_side(da, heads), head_stack(fk, head_of_lane, heads))
            + mm(dn, s_hi, NT)
            + mm(dn, s_lo, NT)
            + dden * ks_ref[i]
        )
        a_hi, a_lo = split(a_old)
        dfk = mm(da, fq_s, TN) + mm(v, a_hi, NT) + mm(v, a_lo, NT) + as_old
        dv = mm(a, dn_s, TN) + mm(fk, a_hi) + mm(fk, a_lo)
        after[...] = a_old + jnp.where(diag, mm(fq, dn, TN), 0.0)
        after_sum[...] = as_old + jnp.sum(fqf * dden, axis=0, keepdims=True)
        dsq = (dfq * fqf).astype(BF16)
        dsk = (dfk * fkf).astype(BF16)
        g_o[...] += mm(rq_ref[rows, :], dsq, TN) + mm(rk_ref[rows, :], dsk, TN)
        dq = turn(mm(dsq, cf_hi, NT) + mm(dsq, cf_lo, NT), cosines, sines, low_half)
        dk = turn(mm(dsk, cf_hi, NT) + mm(dsk, cf_lo, NT), cosines, sines, low_half)
        for j, part in enumerate((dq, dk, dv)):
            part = part.astype(BF16)
            dqkv_o[rows, j * w : (j + 1) * w] = part
            sum_o[:, j * w : (j + 1) * w] += jnp.sum(part.astype(F32), axis=0, keepdims=True)


def attn_bwd_call(units, pads, dao, v, o, rd, fq, fk, rq, rk, s, ks, cf, cos_t, sin_t, hd, parts):
    rows, w = v.shape
    block = rows // parts
    per = block // UNIT
    nseq = units.shape[1]
    smem = pl.BlockSpec(memory_space=pltpu.SMEM)
    sds = jax.ShapeDtypeStruct

    def back(width):
        return pl.BlockSpec((block, width), lambda i: (parts - 1 - i, 0))

    return pl.pallas_call(
        partial(attn_bwd_kernel, nseq, hd, per),
        grid=(parts,),
        in_specs=[smem, smem]
        + [back(w)] * 8
        + [
            pl.BlockSpec((per, 2, w, w), lambda i: (parts - 1 - i, 0, 0, 0)),
            pl.BlockSpec((per, 1, w), lambda i: (parts - 1 - i, 0, 0)),
            whole(cf.shape),
            whole(cos_t.shape),
            whole(sin_t.shape),
        ],
        out_specs=[back(3 * w), whole((w, w)), whole((1, 3 * w))],
        out_shape=[sds((rows, 3 * w), BF16), sds((w, w), F32), sds((1, 3 * w), F32)],
        scratch_shapes=[pltpu.VMEM((w, w), F32), pltpu.VMEM((1, w), F32)],
        compiler_params=params(),
        cost_estimate=pl.CostEstimate(
            flops=10_000_000_000, bytes_accessed=rows * w * 30, transcendentals=0
        ),
        name="attn_bwd",
    )(units, pads, dao, v, o, rd, fq, fk, rq, rk, s, ks, cf, cos_t, sin_t)


def out_kernel(ao, act, wd, wp, out):
    out[...] = (mm(ao[...], wd[...]) + mm(act[...], wp[...])).astype(BF16)


def out_call(ao, act, wd, wp):
    rows, w = ao.shape
    hid, width = wp.shape
    rb = 256
    return pl.pallas_call(
        out_kernel,
        grid=(rows // rb,),
        in_specs=[rows_of(rb, w), rows_of(rb, hid), whole(wd.shape), whole(wp.shape)],
        out_specs=rows_of(rb, width),
        out_shape=jax.ShapeDtypeStruct((rows, width), BF16),
        compiler_params=params(),
        cost_estimate=pl.CostEstimate(
            flops=2 * rows * width * (w + hid), bytes_accessed=rows * (w + hid + width) * 2, transcendentals=0
        ),
        name="branches",
    )(ao, act, wd, wp)


def grad_kernel(g_ref, gp, wd, wp, dao_o, dh_o, sum_o):
    @pl.when(pl.program_id(0) == 0)
    def _():
        sum_o[...] = jnp.zeros_like(sum_o)

    g = g_ref[...]
    dao_o[...] = mm(g, wd[...], NT).astype(BF16)
    dh = (mm(g, wp[...], NT) * gp[...].astype(F32)).astype(BF16)
    dh_o[...] = dh
    sum_o[...] += jnp.sum(dh.astype(F32), axis=0, keepdims=True)


def grad_call(g, gp, wd, wp):
    rows, width = g.shape
    w, hid = wd.shape[0], wp.shape[0]
    rb = 256
    sds = jax.ShapeDtypeStruct
    return pl.pallas_call(
        grad_kernel,
        grid=(rows // rb,),
        in_specs=[rows_of(rb, width), rows_of(rb, hid), whole(wd.shape), whole(wp.shape)],
        out_specs=[rows_of(rb, w), rows_of(rb, hid), whole((1, hid))],
        out_shape=[sds((rows, w), BF16), sds((rows, hid), BF16), sds((1, hid), F32)],
        compiler_params=params(),
        cost_estimate=pl.CostEstimate(
            flops=2 * rows * width * (w + hid), bytes_accessed=rows * (w + 2 * hid + width) * 2, transcendentals=0
        ),
        name="branch_grads",
    )(g, gp, wd, wp)


def back_kernel(x, dqkv, dh, vec, wqkv, wfc, e_o, sum_o):
    @pl.when(pl.program_id(0) == 0)
    def _():
        sum_o[...] = jnp.zeros_like(sum_o)

    xh, _ = norm_rows(x[...].astype(F32))
    da = mm(dqkv[...], wqkv[...], NT)
    dm = mm(dh[...], wfc[...], NT)
    e_o[...] = (da * vec[0:1, :] + dm * vec[2:3, :]).astype(BF16)
    for j, part in enumerate((da * xh, da, dm * xh, dm)):
        sum_o[j : j + 1, :] += jnp.sum(part, axis=0, keepdims=True)


def back_call(x, dqkv, dh, vec, wqkv, wfc):
    rows, width = x.shape
    cols, hid = dqkv.shape[1], dh.shape[1]
    rb = 256
    sds = jax.ShapeDtypeStruct
    return pl.pallas_call(
        back_kernel,
        grid=(rows // rb,),
        in_specs=[
            rows_of(rb, width),
            rows_of(rb, cols),
            rows_of(rb, hid),
            whole(vec.shape),
            whole(wqkv.shape),
            whole(wfc.shape),
        ],
        out_specs=[rows_of(rb, width), whole((4, width))],
        out_shape=[sds((rows, width), BF16), sds((4, width), F32)],
        compiler_params=params(),
        cost_estimate=pl.CostEstimate(
            flops=2 * rows * width * (cols + hid), bytes_accessed=rows * (cols + hid + 2 * width) * 2, transcendentals=0
        ),
        name="norm_grads",
    )(x, dqkv, dh, vec, wqkv, wfc)


def both(a, b):
    return (a.astype(F32) + b.astype(F32)).astype(BF16)


def line_sum(pieces):
    index = lax.axis_index("batch")
    core, z = index % 2, index // 2
    mid = (z == 1) | (z == 2)
    swap = [(i, i ^ 1) for i in range(8)]
    outer = [(0, 2), (2, 0), (1, 3), (3, 1), (4, 6), (6, 4), (5, 7), (7, 5)]
    inner = [(2, 4), (4, 2), (3, 5), (5, 3)]
    count = len(pieces)
    mine, totals, done = {}, {}, {}
    for k in range(count + 2):
        if k < count:
            own = lax.dynamic_index_in_dim(pieces[k], core, 0, keepdims=False)
            other = lax.dynamic_index_in_dim(pieces[k], 1 - core, 0, keepdims=False)
            mine[k] = both(own, lax.ppermute(other, "batch", swap))
        if k < 2:
            send = mine[k]
        elif k < count:
            send = jnp.where(mid, totals[k - 2], mine[k])
        else:
            send = totals[k - 2]
        got = lax.ppermute(send, "batch", outer)
        if k < count:
            part = both(mine[k], got)
            totals[k] = both(part, lax.ppermute(part, "batch", inner))
        if k >= 2:
            total = jnp.where(mid, totals[k - 2], got)
            far = lax.ppermute(total, "batch", swap)
            done[k - 2] = jnp.stack([jnp.where(core == 0, total, far), jnp.where(core == 0, far, total)])
    return [done[k] for k in range(count)]


def sum_weight_grads(proj, fc, dense, qkv, n_batch):
    hid, width = proj.shape
    w = dense.shape[0]
    if n_batch != 8 or fc.shape != proj.shape or 4 * w != width:
        return tuple(lax.psum(a, "batch") for a in (proj, fc, dense, qkv))
    piece = (2, width // 4, width)
    half = width // 2
    last = jnp.concatenate([dense, qkv[:w]])
    pieces = [proj[:half], proj[half:], fc[:half], fc[half:], last, qkv[w:]]
    p0, p1, f0, f1, dq, q = (a.reshape(half, width) for a in line_sum([a.reshape(piece) for a in pieces]))
    return (
        jnp.concatenate([p0, p1]),
        jnp.concatenate([f0, f1]),
        dq[:w],
        jnp.concatenate([dq[w:], q]),
    )


def cosine_table(dimension):
    spatial = jnp.arange(dimension, dtype=F32)[:, None]
    frequency = jnp.arange(dimension, dtype=F32)[None, :]
    dct_table = jnp.cos(math.pi * (2.0 * spatial + 1.0) * frequency / (2.0 * dimension)) * math.sqrt(
        2.0 / dimension
    )
    return jnp.where(frequency == 0.0, dct_table * math.sqrt(0.5), dct_table)


def turn_tables(rows, hd):
    half = ROT // 2
    inverse_freq = jnp.exp(-math.log(10000.0) * 2.0 * jnp.arange(half, dtype=F32) / ROT)
    angles = jnp.arange(rows, dtype=F32)[:, None] * inverse_freq[None, :]
    cosines, sines = jnp.cos(angles), jnp.sin(angles)
    ones, zeros = jnp.ones((rows, hd - ROT), F32), jnp.zeros((rows, hd - ROT), F32)
    reps = 128 // hd
    return (
        jnp.tile(jnp.concatenate([cosines, cosines, ones], axis=1), (1, reps)),
        jnp.tile(jnp.concatenate([-sines, sines, zeros], axis=1), (1, reps)),
    )


def body(
    tokens,
    output_grad,
    attn_norm_gain,
    attn_norm_bias,
    mlp_norm_gain,
    mlp_norm_bias,
    qkv_weight,
    qkv_bias,
    dense_weight,
    dense_bias,
    fc_weight,
    fc_bias,
    proj_weight,
    feature_weight,
    seq_units,
    pad_tokens,
):
    rows_dev, width = tokens.shape
    parts = lax.axis_size("tensor")
    n_batch = lax.axis_size("batch")
    rows = rows_dev * parts
    heads, hd, _ = feature_weight.shape
    w = heads * hd
    hid = fc_weight.shape[1]

    vec = jnp.stack([attn_norm_gain, attn_norm_bias, mlp_norm_gain, mlp_norm_bias]).astype(F32)
    wqkv = qkv_weight.reshape(width, heads, 3, hd).transpose(0, 2, 1, 3).reshape(width, 3 * w)
    bqkv = qkv_bias.reshape(heads, 3, hd).transpose(1, 0, 2).reshape(1, 3 * w).astype(F32)
    dct = cosine_table(hd)
    cf = jnp.einsum("de,hem->hdm", dct, feature_weight.astype(F32), precision=lax.Precision.HIGHEST)
    eye = jnp.eye(heads, dtype=F32)
    cf_bd = (cf[:, :, None, :] * eye[:, None, :, None]).reshape(w, w)
    cf_pair = jnp.stack(split(cf_bd))
    cos_t, sin_t = turn_tables(rows, hd)

    x_all = lax.all_gather(tokens, "tensor", axis=0, tiled=True)
    g_all = lax.all_gather(output_grad, "tensor", axis=0, tiled=True)

    lna, lnm, qk, v, act, gp = fwd_call(
        x_all, vec, wqkv, bqkv, fc_weight, fc_bias.astype(F32).reshape(1, hid)
    )
    ao, o, rd, fq, fk, rq, rk, s, ks = attn_fwd_call(
        seq_units, pad_tokens, qk, v, cf_pair, cos_t, sin_t, hd, parts
    )
    branch = lax.psum_scatter(
        out_call(ao, act, dense_weight, proj_weight), "tensor", scatter_dimension=0, tiled=True
    )
    x_own = tokens.astype(F32)
    output = (x_own + branch.astype(F32) + dense_bias.astype(F32)).astype(BF16)

    dao, dh, fc_bias_sum = grad_call(g_all, gp, dense_weight, proj_weight)
    proj_grad = mm(act, g_all, TN).astype(BF16)
    dense_grad = mm(ao, g_all, TN).astype(BF16)
    fc_grad = mm(lnm, dh, TN).astype(BF16)
    dqkv, feat, qkv_bias_sum = attn_bwd_call(
        seq_units, pad_tokens, dao, v, o, rd, fq, fk, rq, rk, s, ks, cf_pair, cos_t, sin_t, hd, parts
    )
    qkv_grad = mm(dqkv, lna, TN).astype(BF16)
    e_part, norm_sums = back_call(x_all, dqkv, dh, vec, wqkv, fc_weight)
    e = lax.psum_scatter(e_part, "tensor", scatter_dimension=0, tiled=True).astype(F32)
    x_hat, inv_std = norm_rows(x_own)
    g_own = output_grad.astype(F32)
    tokens_grad = (
        g_own
        + inv_std
        * (e - jnp.mean(e, axis=-1, keepdims=True) - x_hat * jnp.mean(e * x_hat, axis=-1, keepdims=True))
    ).astype(BF16)

    proj_grad, fc_grad, dense_grad, qkv_grad = sum_weight_grads(
        proj_grad, fc_grad, dense_grad, qkv_grad, n_batch
    )
    proj_grad, fc_grad, dense_grad = (a.astype(F32) for a in (proj_grad, fc_grad, dense_grad))
    qkv_grad = (
        qkv_grad.reshape(3, heads, hd, width).transpose(3, 1, 0, 2).reshape(width, 3 * w).astype(F32)
    )

    feat_blocks = jnp.stack([feat[h * hd : (h + 1) * hd, h * hd : (h + 1) * hd] for h in range(heads)])
    feat_sum, qkv_bias_sum, fc_bias_sum = lax.psum((feat_blocks, qkv_bias_sum, fc_bias_sum), "batch")
    norm_sums, dense_bias_sum = lax.psum((norm_sums, jnp.sum(g_own, axis=0)), ("batch", "tensor"))
    feature_grad = jnp.einsum("de,hdm->hem", dct, feat_sum, precision=lax.Precision.HIGHEST)
    qkv_bias_grad = qkv_bias_sum.reshape(3, heads, hd).transpose(1, 0, 2).reshape(3 * w)
    return (
        output,
        tokens_grad,
        norm_sums[0],
        norm_sums[1],
        norm_sums[2],
        norm_sums[3],
        qkv_grad,
        qkv_bias_grad,
        dense_grad,
        dense_bias_sum,
        fc_grad,
        fc_bias_sum.reshape(hid),
        proj_grad,
        feature_grad,
    )


def solution(mesh):
    rows = P(("batch", "tensor"), None)
    placed = (
        rows,
        rows,
        P(),
        P(),
        P(),
        P(),
        P(None, "tensor"),
        P("tensor"),
        P("tensor", None),
        P(),
        P(None, "tensor"),
        P("tensor"),
        P("tensor", None),
        P("tensor", None, None),
        P("batch", None),
        P("batch", None),
    )
    return jax.shard_map(
        body,
        mesh=mesh,
        in_specs=placed,
        out_specs=(
            rows,
            rows,
            P(),
            P(),
            P(),
            P(),
            P(None, "tensor"),
            P("tensor"),
            P("tensor", None),
            P(),
            P(None, "tensor"),
            P("tensor"),
            P("tensor", None),
            P("tensor", None, None),
        ),
        check_vma=False,
    )
```

time: 751 us -> 367 us (0.49)
  waiting for transfers between devices: 391 us -> 92.7 us
  matrix products: 157 us -> 16.2 us
  Pallas kernels: 0 us -> 71.2 us
  local copies, waits for them, and re-layouts: 79.5 us -> 24.6 us
  starting transfers between devices: 0.41 us -> 48.7 us
    psum x1, waiting for transfers between devices: 218 us -> 0.01 us  [body(): lax.psum((feat_blocks, qkv_bias_sum, fc_bias_sum), 'batch')]
    dot_general x41 -> x6, matrix products: 157 us -> 16.2 us  [the longest x4 13.8 us: mm(): return lax.dot_general(a, b, dims, preferred_element_type=F32)]
    reduce_scatter x2, waiting for transfers between devices: 128 us -> 0.02 us  [the longest x1 0.02 us: body(): lax.psum_scatter(out_call(ao, act, dense_weight, proj_weight), 'tensor',...]
    pallas_call x0 -> x6, Pallas kernels: none -> 71.2 us  [the longest x1 14.7 us: attn_bwd_call(): pl.pallas_call(partial(attn_bwd_kernel, nseq, hd, per), grid=(parts,), in...]
    ppermute x0 -> x26, starting transfers between devices: none -> 48.3 us  [the longest x8 40.8 us: line_sum(): got = lax.ppermute(send, 'batch', outer)]
    ppermute x0 -> x26, waiting for transfers between devices: none -> 36.3 us  [the longest x8 36.2 us: line_sum(): got = lax.ppermute(send, 'batch', outer)]
    reshape x7 -> x4, local copies, waits for them, and re-layouts: 25.3 us -> 1.75 us  [the longest x1 1.59 us: body(): qkv_weight.reshape(width, heads, 3, hd).transpose(0, 2, 1, 3)]
    unnamed x138 -> x57, local copies, waits for them, and re-layouts: 22.9 us -> 10.2 us
  transfers between devices with their start and end apart: 6 -> 31, of which waited for: 4 -> 6; matrix products, arithmetic and copies ran while one was open for 28% -> 19% of each run, Pallas kernels for 0% -> 13%
where the time goes in v1:
time: 367 us; the launch traced here: 365 us
  waiting for transfers between devices  92.7 us (25%)
  Pallas kernels  71.2 us (19%)
  blocking collectives  61.1 us (17%)
  starting transfers between devices  48.7 us (13%)
  other arithmetic  35.9 us (10%)
  local copies, waits for them, and re-layouts  24.6 us (7%)
  matrix products  16.2 us (4%)
  between operations  14.7 us (4%)
    ppermute x8, starting transfers between devices, line_sum(): got = lax.ppermute(send, 'batch', outer)  40.8 us
    psum x1, blocking collectives, body(): lax.psum((norm_sums, jnp.sum(g_own, axis=0)), ('batch', 'tensor'))  39.9 us
    ppermute x8, waiting for transfers between devices, line_sum(): got = lax.ppermute(send, 'batch', outer)  36.2 us
    all_gather x1, waiting for transfers between devices, body(): x_all = lax.all_gather(tokens, 'tensor', axis=0, tiled=True)  35.1 us
    psum x1, blocking collectives, body(): lax.psum((feat_blocks, qkv_bias_sum, fc_bias_sum), 'batch')  21.2 us
    all_gather x1, waiting for transfers between devices, body(): g_all = lax.all_gather(output_grad, 'tensor', axis=0, tiled=True)  19.9 us
    pallas_call x1, Pallas kernels, attn_bwd_call(): pl.pallas_call(partial(attn_bwd_kernel, nseq, hd, per), grid=(parts,), in...  14.7 us
    pallas_call x1, Pallas kernels, fwd_call(): pl.pallas_call(fwd_kernel, grid=(rows // rb,), in_specs=[rows_of(rb, widt...  14.2 us
  transfers between devices with their start and end apart: 31, of which 6 were waited for; matrix products, arithmetic and copies ran while one was open for 19% of the time, Pallas kernels for 13%

profile of v1, /device:TPU:0, one launch (start us, length us, event | category | flops | bytes accessed | tf_op | source)
XLA Modules:
  0.0 365.1 jit_solution(12947496345657259487)
XLA Ops:
  21.6 35.1 %all-gather.3.cloned.1.call-done.x = bf16[1536,1024]{1,0:T(8,128)(2,1)} async-done(((bf16[384,1024]{1,0:T(8,128)(2,1)}), bf16[1536,1024]{1,0:T(8,128)(2,1)}) %all-gather.3.cloned.1.call-update) | async-done | bytes 3145744 | tf_op jit(solution)/shard_map/all_gather | solution.py:556
  56.6 14.2 %norm_qkv_fc.1 = (bf16[1536,1024]{1,0:T(8,128)(2,1)}, bf16[1536,1024]{1,0:T(8,128)(2,1)}, f32[1536,512]{1,0:T(8,128)}, bf16[1536,256]{1,0:T(8,128)(2,1)}, bf16[1...) custom-call(bf16[1536,1024]{1,0:T(8,128)(2,1)} %all-gather.3.cloned.1.call-done.x, f32[4,1024]{1,0:T(4,128)} %maximum_convert_fusion.2.vec, ...), custom_call_target="tpu_custom_call" | custom-call | flops 5637144576 | bytes 31457280 | tf_op jit(solution)/shard_map/norm_qkv_fc/pallas_call | solution.py:75
  70.9 11.7 %attn_fwd.1 = (bf16[1536,256]{1,0:T(8,128)(2,1)}, f32[1536,256]{1,0:T(8,128)}, f32[1536,256]{1,0:T(8,128)}, bf16[1536,256]{1,0:T(8,128)(2,1)}, bf16[1536,256]{1,...) custom-call(s32[1,4]{1,0:T(1,128)} %units.3, ...), custom_call_target="tpu_custom_call" | custom-call | flops 6000000000 | bytes 9437184 | tf_op jit(solution)/shard_map/attn_fwd/pallas_call | solution.py:219
  82.6 19.9 %all-gather.5.cloned.1.call-done.g_ref = bf16[1536,1024]{1,0:T(8,128)(2,1)} async-done(((bf16[384,1024]{1,0:T(8,128)(2,1)}), bf16[1536,1024]{1,0:T(8,128)(2,1)}) %all-gather.5.cloned.1.call-update) | async-done | bytes 3145744 | tf_op jit(solution)/shard_map/all_gather | solution.py:557
  102.5 9.6 %branch_grads.1 = (bf16[1536,256]{1,0:T(8,128)(2,1)}, bf16[1536,1024]{1,0:T(8,128)(2,1)}, f32[1,1024]{1,0:T(1,128)}) custom-call(bf16[1536,1024]{1,0:T(8,128)(2,1)} %all-gather.5.cloned.1.call-done.g_ref, bf16[1536,1024]{1,0:T(8,128)(2,1)} %get-tuple-element.41.gp, bf16[256,1024]{1,0:T(8,128)(2,1)} %wd.3, bf16[1024,1024]{1,0:T(8,128)(2,1)} %wp.3), custom_call_target="tpu_custom_call" | custom-call | flops 4026531840 | bytes 10223616 | tf_op jit(solution)/shard_map/branch_grads/pallas_call | solution.py:392
  112.1 14.7 %attn_bwd.1 = (bf16[1536,768]{1,0:T(8,128)(2,1)}, f32[256,256]{1,0:T(8,128)}, f32[1,768]{1,0:T(1,128)}) custom-call(s32[1,4]{1,0:T(1,128)} %units.3, s32[1,4]{1,0:T(1,128)} %pads.3, bf16[1536,256]{1,0:T(8,128)(2,1)} %get-tuple-element.42.dao, bf16[1536,256]{1,0:T(8,128)(2,1)} %get-tuple-element.38.v_ref, f32[1536,256]{1,0:T(8,128)} %get-tuple-element.43.o_ref, ...), custom_call_target="tpu_custom_call" | custom-call | flops 10000000000 | bytes 11796480 | tf_op jit(solution)/shard_map/attn_bwd/pallas_call | solution.py:330
  128.4 12.1 %norm_grads.1 = (bf16[1536,1024]{1,0:T(8,128)(2,1)}, f32[4,1024]{1,0:T(4,128)}) custom-call(bf16[1536,1024]{1,0:T(8,128)(2,1)} %all-gather.3.cloned.1.call-done.x, bf16[1536,768]{1,0:T(8,128)(2,1)} %get-tuple-element.51.dqkv, bf16[1536,1024]{1,0:T(8,128)(2,1)} %get-tuple-element.52.dh, f32[4,1024]{1,0:T(4,128)} %maximum_convert_fusion.2.vec, ...), custom_call_target="tpu_custom_call" | custom-call | flops 5637144576 | bytes 11796480 | tf_op jit(solution)/shard_map/norm_grads/pallas_call | solution.py:424
  141.6 6.5 %convolution_convert_fusion = bf16[1024,1024]{1,0:T(8,128)(2,1)S(1)} fusion(bf16[1536,1024]{1,0:T(8,128)(2,1)} %get-tuple-element.40.act, bf16[1536,1024]{1,0:T(8,128)(2,1)} %all-gather.5.cloned.1.call-done.g_ref), kind=kOutput, calls=%fused_computation.11 | convolution fusion | flops 3222274048 | bytes 8388608 | tf_op jit(solution)/shard_map/dot_general | solution.py:24
  150.0 2.7 convolution_convert_fusion.2
  152.9 3.7 %convolution_convert_fusion.1 = bf16[1024,1024]{1,0:T(8,128)(2,1)S(1)} fusion(bf16[1536,1024]{1,0:T(8,128)(2,1)S(1)} %copy-done.25, bf16[1536,1024]{1,0:T(8,128)(2,1)S(1)} %copy-done.26), kind=kOutput, calls=%fused_computation.12 | convolution fusion | flops 3222274048 | bytes 8388608 | tf_op jit(solution)/shard_map/dot_general | solution.py:24
  164.1 11.0 %collective-permute-done.3 = bf16[256,1024]{1,0:T(8,128)(2,1)S(1)} collective-permute-done((bf16[256,1024]{1,0:T(8,128)(2,1)S(1)}, bf16[256,1024]{1,0:T(8,128)(2,1)S(1)}, u32[]{:S(2)}, u32[]{:S(2)}) %collective-permute-start.3) | collective-permute-done | bytes 524320 | tf_op jit(solution)/shard_map/ppermute | solution.py:469
  177.6 8.9 %branches.1 = bf16[1536,1024]{1,0:T(8,128)(2,1)} custom-call(bf16[1536,256]{1,0:T(8,128)(2,1)} %get-tuple-element.39.ao, bf16[1536,1024]{1,0:T(8,128)(2,1)} %get-tuple-element.40.act, bf16[256,1024]{1,0:T(8,128)(2,1)} %wd.3, bf16[1024,1024]{1,0:T(8,128)(2,1)} %wp.3), custom_call_target="tpu_custom_call" | custom-call | flops 4026531840 | bytes 7077888 | tf_op jit(solution)/shard_map/branches/pallas_call | solution.py:361
  192.0 4.5 %collective-permute-start.5 = (bf16[256,1024]{1,0:T(8,128)(2,1)}, bf16[256,1024]{1,0:T(8,128)(2,1)}, u32[]{:S(2)}, u32[]{:S(2)}) collective-permute-start(bf16[256,1024]{1,0:T(8,128)(2,1)} %broadcast_select_fusion.9), channel_id=1, source_target_pairs={{0,8},{8,0},{4,12},{12,4},{16,24},{24,16},{20,28},{28,20},{1,9},{9... | collective-permute-start | bytes 1572872 | tf_op jit(solution)/shard_map/ppermute | solution.py:469
  197.6 21.2 %all-reduce.1 = (f32[768]{0:T(1024)}, f32[1024]{0:T(1024)}) all-reduce(f32[768]{0:T(1024)S(1)} %reshape.232, f32[1024]{0:T(1024)S(1)} %bitcast.155), channel_id=1, replica_groups=mesh['batch'=8,'tensor'=4] {'batch'}, use_global_device_ids=true, to_apply=%region_7.8 | all-reduce | flops 1792 | bytes 14336 | tf_op jit(solution)/shard_map/psum | solution.py:598
  228.4 6.9 %collective-permute-done.16 = bf16[256,1024]{1,0:T(8,128)(2,1)S(1)} collective-permute-done((bf16[256,1024]{1,0:T(8,128)(2,1)S(1)}, bf16[256,1024]{1,0:T(8,128)(2,1)S(1)}, u32[]{:S(2)}, u32[]{:S(2)}) %collective-permute-start.16) | collective-permute-done | bytes 524320 | tf_op jit(solution)/shard_map/ppermute | solution.py:469
  240.4 7.3 %collective-permute-start.7 = (bf16[256,1024]{1,0:T(8,128)(2,1)S(1)}, bf16[256,1024]{1,0:T(8,128)(2,1)S(1)}, u32[]{:S(2)}, u32[]{:S(2)}) collective-permute-start(bf16[256,1024]{1,0:T(8,128)(2,1)S(1)} %broadcast_select_fusion.8), channel_id=1, source_target_pairs={{0,8},{8,0},{4,12},{12,4},{16,24},{24,16},{20,28},{28,20},{1,9},{9... | collective-permute-start | bytes 1572872 | tf_op jit(solution)/shard_map/ppermute | solution.py:469
  249.1 9.4 %collective-permute-start.18 = (bf16[256,1024]{1,0:T(8,128)(2,1)S(1)}, bf16[256,1024]{1,0:T(8,128)(2,1)S(1)}, u32[]{:S(2)}, u32[]{:S(2)}) collective-permute-start(bf16[256,1024]{1,0:T(8,128)(2,1)S(1)} %broadcast_select_fusion.5), channel_id=1, source_target_pairs={{0,8},{8,0},{4,12},{12,4},{16,24},{24,16},{20,28},{28,20},{1,9},{9... | collective-permute-start | bytes 1572872 | tf_op jit(solution)/shard_map/ppermute | solution.py:469
  263.7 6.7 %collective-permute-done.18 = bf16[256,1024]{1,0:T(8,128)(2,1)S(1)} collective-permute-done((bf16[256,1024]{1,0:T(8,128)(2,1)S(1)}, bf16[256,1024]{1,0:T(8,128)(2,1)S(1)}, u32[]{:S(2)}, u32[]{:S(2)}) %collective-permute-start.18) | collective-permute-done | bytes 524320 | tf_op jit(solution)/shard_map/ppermute | solution.py:469
  273.0 6.9 %collective-permute-start.9 = (bf16[256,1024]{1,0:T(8,128)(2,1)S(1)}, bf16[256,1024]{1,0:T(8,128)(2,1)S(1)}, u32[]{:S(2)}, u32[]{:S(2)}) collective-permute-start(bf16[256,1024]{1,0:T(8,128)(2,1)S(1)} %add_convert_fusion.6), channel_id=1, source_target_pairs={{0,8},{8,0},{4,12},{12,4},{16,24},{24,16},{20,28},{28,20},{1,9},{9... | collective-permute-start | bytes 1572872 | tf_op jit(solution)/shard_map/ppermute | solution.py:469
  280.1 10.6 %collective-permute-start.20 = (bf16[256,1024]{1,0:T(8,128)(2,1)S(1)}, bf16[256,1024]{1,0:T(8,128)(2,1)S(1)}, u32[]{:S(2)}, u32[]{:S(2)}) collective-permute-start(bf16[256,1024]{1,0:T(8,128)(2,1)S(1)} %add_convert_fusion), channel_id=1, source_target_pairs={{0,8},{8,0},{4,12},{12,4},{16,24},{24,16},{20,28},{28,20},{1,9},{9... | collective-permute-start | bytes 1572872 | tf_op jit(solution)/shard_map/ppermute | solution.py:469
  291.0 11.5 %collective-permute-done.20 = bf16[256,1024]{1,0:T(8,128)(2,1)S(1)} collective-permute-done((bf16[256,1024]{1,0:T(8,128)(2,1)S(1)}, bf16[256,1024]{1,0:T(8,128)(2,1)S(1)}, u32[]{:S(2)}, u32[]{:S(2)}) %collective-permute-start.20) | collective-permute-done | bytes 524320 | tf_op jit(solution)/shard_map/ppermute | solution.py:469
  309.5 3.5 copy.59
  315.0 3.0 convert_reduce_fusion.2
  318.1 39.9 %all-reduce = (f32[4,1024]{1,0:T(4,128)S(1)}, f32[1024]{0:T(1024)}) all-reduce(f32[4,1024]{1,0:T(4,128)S(1)} %copy-done.11, f32[1024]{0:T(1024)S(1)} %get-tuple-element.126), channel_id=1, replica_groups=mesh['batch'=8,'tensor'=4] {'batch','tensor'}, use_global_device_ids=true, to_apply=%region_6.7 | all-reduce | flops 5120 | bytes 40960 | tf_op jit(solution)/shard_map/psum | solution.py:599
  (207 shorter events, 68.9 us)
Async XLA Ops:
  7.2 49.4 %all-gather.3.cloned.1.call-start = ((), (), s32[]{:S(2)}) async-start(), calls=%async_computation.2 | async-start | bytes 3932160 | tf_op jit(solution)/shard_map/all_gather | solution.py:556
  7.9 94.6 %all-gather.5.cloned.1.call-start = ((), (), s32[]{:S(2)}) async-start(), calls=%async_computation.4 | async-start | bytes 3932160 | tf_op jit(solution)/shard_map/all_gather | solution.py:557
  8.7 210.1 %all-reduce.4.cloned.1.call-start = ((), (), s32[]{:S(2)}) async-start(), calls=%async_computation.6 | async-start | bytes 262144 | tf_op jit(solution)/shard_map/psum | solution.py:598
  128.4 184.7 %reduce-scatter.5.cloned.1.call-start = ((), (), s32[]{:S(2)}) async-start(), calls=%async_computation.5 | async-start | bytes 3932160 | tf_op jit(solution)/shard_map/reduce_scatter | solution.py:580
  140.6 174.5 %reduce-scatter.3.cloned.1.call-start = ((), (), s32[]{:S(2)}) async-start(), calls=%async_computation.3 | async-start | bytes 3932160 | tf_op jit(solution)/shard_map/reduce_scatter | solution.py:565
  157.9 31.5 %collective-permute-start.1 = (bf16[256,1024]{1,0:T(8,128)(2,1)}, bf16[256,1024]{1,0:T(8,128)(2,1)}, u32[]{:S(2)}, u32[]{:S(2)}) collective-permute-start(bf16[256,1024]{1,0:T(8,128)(2,1)} %dynamic-slice_bitcast_fusion.4), channel_id=1, source_target_pairs={{0,4},{4,0},{8,12},{12,8},{16,20},{20,16},{24,28},{28,24},{1,5},{5... | collective-permute-start | bytes 1572872 | tf_op jit(solution)/shard_map/ppermute | solution.py:462
  159.3 63.2 %collective-permute-start.12 = (bf16[256,1024]{1,0:T(8,128)(2,1)}, bf16[256,1024]{1,0:T(8,128)(2,1)}, u32[]{:S(2)}, u32[]{:S(2)}) collective-permute-start(bf16[256,1024]{1,0:T(8,128)(2,1)} %dynamic-slice_bitcast_fusion.1), channel_id=1, source_target_pairs={{0,4},{4,0},{8,12},{12,8},{16,20},{20,16},{24,28},{28,24},{1,5},{5... | collective-permute-start | bytes 1572872 | tf_op jit(solution)/shard_map/ppermute | solution.py:462
  159.5 15.6 %collective-permute-start.3 = (bf16[256,1024]{1,0:T(8,128)(2,1)S(1)}, bf16[256,1024]{1,0:T(8,128)(2,1)S(1)}, u32[]{:S(2)}, u32[]{:S(2)}) collective-permute-start(bf16[256,1024]{1,0:T(8,128)(2,1)S(1)} %fusion.13), channel_id=1, source_target_pairs={{0,8},{8,0},{4,12},{12,4},{16,24},{24,16},{20,28},{28,20},{1,9},{9... | collective-permute-start | bytes 1572872 | tf_op jit(solution)/shard_map/ppermute | solution.py:469
  163.1 75.6 %collective-permute-start = (bf16[256,1024]{1,0:T(8,128)(2,1)}, bf16[256,1024]{1,0:T(8,128)(2,1)}, u32[]{:S(2)}, u32[]{:S(2)}) collective-permute-start(bf16[256,1024]{1,0:T(8,128)(2,1)} %dynamic-slice_bitcast_fusion.5), channel_id=1, source_target_pairs={{0,4},{4,0},{8,12},{12,8},{16,20},{20,16},{24,28},{28,24},{1,5},{5... | collective-permute-start | bytes 1572872 | tf_op jit(solution)/shard_map/ppermute | solution.py:462
  163.5 22.9 %collective-permute-start.14 = (bf16[256,1024]{1,0:T(8,128)(2,1)S(1)}, bf16[256,1024]{1,0:T(8,128)(2,1)}, u32[]{:S(2)}, u32[]{:S(2)}) collective-permute-start(bf16[256,1024]{1,0:T(8,128)(2,1)S(1)} %fusion.10), channel_id=1, source_target_pairs={{0,8},{8,0},{4,12},{12,4},{16,24},{24,16},{20,28},{28,20},{1,9},{9... | collective-permute-start | bytes 1572872 | tf_op jit(solution)/shard_map/ppermute | solution.py:469
  176.1 13.3 %collective-permute-start.4 = (bf16[256,1024]{1,0:T(8,128)(2,1)}, bf16[256,1024]{1,0:T(8,128)(2,1)}, u32[]{:S(2)}, u32[]{:S(2)}) collective-permute-start(bf16[256,1024]{1,0:T(8,128)(2,1)} %add_convert_fusion.11), channel_id=1, source_target_pairs={{8,16},{16,8},{12,20},{20,12},{9,17},{17,9},{13,21},{21,13},{10,18... | collective-permute-start | bytes 1572872 | tf_op jit(solution)/shard_map/ppermute | solution.py:472
  187.9 34.6 %collective-permute-start.15 = (bf16[256,1024]{1,0:T(8,128)(2,1)S(1)}, bf16[256,1024]{1,0:T(8,128)(2,1)}, u32[]{:S(2)}, u32[]{:S(2)}) collective-permute-start(bf16[256,1024]{1,0:T(8,128)(2,1)S(1)} %add_convert_fusion.5), channel_id=1, source_target_pairs={{8,16},{16,8},{12,20},{20,12},{9,17},{17,9},{13,21},{21,13},{10,18... | collective-permute-start | bytes 1572872 | tf_op jit(solution)/shard_map/ppermute | solution.py:472
  192.0 32.4 %collective-permute-start.5 = (bf16[256,1024]{1,0:T(8,128)(2,1)}, bf16[256,1024]{1,0:T(8,128)(2,1)}, u32[]{:S(2)}, u32[]{:S(2)}) collective-permute-start(bf16[256,1024]{1,0:T(8,128)(2,1)} %broadcast_select_fusion.9), channel_id=1, source_target_pairs={{0,8},{8,0},{4,12},{12,4},{16,24},{24,16},{20,28},{28,20},{1,9},{9... | collective-permute-start | bytes 1572872 | tf_op jit(solution)/shard_map/ppermute | solution.py:469
  197.3 50.3 %collective-permute-start.11 = (bf16[256,1024]{1,0:T(8,128)(2,1)}, bf16[256,1024]{1,0:T(8,128)(2,1)}, u32[]{:S(2)}, u32[]{:S(2)}) collective-permute-start(bf16[256,1024]{1,0:T(8,128)(2,1)} %dynamic-slice_bitcast_fusion.2), channel_id=1, source_target_pairs={{0,4},{4,0},{8,12},{12,8},{16,20},{20,16},{24,28},{28,24},{1,5},{5... | collective-permute-start | bytes 1572872 | tf_op jit(solution)/shard_map/ppermute | solution.py:462
  224.3 11.0 %collective-permute-start.16 = (bf16[256,1024]{1,0:T(8,128)(2,1)S(1)}, bf16[256,1024]{1,0:T(8,128)(2,1)S(1)}, u32[]{:S(2)}, u32[]{:S(2)}) collective-permute-start(bf16[256,1024]{1,0:T(8,128)(2,1)S(1)} %broadcast_select_fusion.6), channel_id=1, source_target_pairs={{0,8},{8,0},{4,12},{12,4},{16,24},{24,16},{20,28},{28,20},{1,9},{9... | collective-permute-start | bytes 1572872 | tf_op jit(solution)/shard_map/ppermute | solution.py:469
  226.2 32.3 %collective-permute-start.24 = (bf16[256,1024]{1,0:T(8,128)(2,1)S(1)}, bf16[256,1024]{1,0:T(8,128)(2,1)S(1)}, u32[]{:S(2)}, u32[]{:S(2)}) collective-permute-start(bf16[256,1024]{1,0:T(8,128)(2,1)S(1)} %broadcast_select_fusion.1), channel_id=1, source_target_pairs={{0,4},{4,0},{8,12},{12,8},{16,20},{20,16},{24,28},{28,24},{1,5},{5... | collective-permute-start | bytes 1572872 | tf_op jit(solution)/shard_map/ppermute | solution.py:475
  227.7 11.1 %collective-permute-start.6 = (bf16[256,1024]{1,0:T(8,128)(2,1)S(1)}, bf16[256,1024]{1,0:T(8,128)(2,1)S(1)}, u32[]{:S(2)}, u32[]{:S(2)}) collective-permute-start(bf16[256,1024]{1,0:T(8,128)(2,1)S(1)} %add_convert_fusion.9), channel_id=1, source_target_pairs={{8,16},{16,8},{12,20},{20,12},{9,17},{17,9},{13,21},{21,13},{10,18... | collective-permute-start | bytes 1572872 | tf_op jit(solution)/shard_map/ppermute | solution.py:472
  238.7 19.8 %collective-permute-start.25 = (bf16[256,1024]{1,0:T(8,128)(2,1)S(1)}, bf16[256,1024]{1,0:T(8,128)(2,1)S(1)}, u32[]{:S(2)}, u32[]{:S(2)}) collective-permute-start(bf16[256,1024]{1,0:T(8,128)(2,1)S(1)} %broadcast_select_fusion), channel_id=1, source_target_pairs={{0,4},{4,0},{8,12},{12,8},{16,20},{20,16},{24,28},{28,24},{1,5},{5... | collective-permute-start | bytes 1572872 | tf_op jit(solution)/shard_map/ppermute | solution.py:475
  240.4 20.9 %collective-permute-start.7 = (bf16[256,1024]{1,0:T(8,128)(2,1)S(1)}, bf16[256,1024]{1,0:T(8,128)(2,1)S(1)}, u32[]{:S(2)}, u32[]{:S(2)}) collective-permute-start(bf16[256,1024]{1,0:T(8,128)(2,1)S(1)} %broadcast_select_fusion.8), channel_id=1, source_target_pairs={{0,8},{8,0},{4,12},{12,4},{16,24},{24,16},{20,28},{28,20},{1,9},{9... | collective-permute-start | bytes 1572872 | tf_op jit(solution)/shard_map/ppermute | solution.py:469
  249.1 21.3 %collective-permute-start.18 = (bf16[256,1024]{1,0:T(8,128)(2,1)S(1)}, bf16[256,1024]{1,0:T(8,128)(2,1)S(1)}, u32[]{:S(2)}, u32[]{:S(2)}) collective-permute-start(bf16[256,1024]{1,0:T(8,128)(2,1)S(1)} %broadcast_select_fusion.5), channel_id=1, source_target_pairs={{0,8},{8,0},{4,12},{12,4},{16,24},{24,16},{20,28},{28,20},{1,9},{9... | collective-permute-start | bytes 1572872 | tf_op jit(solution)/shard_map/ppermute | solution.py:469
  261.6 29.1 %collective-permute-start.22 = (bf16[256,1024]{1,0:T(8,128)(2,1)S(1)}, bf16[256,1024]{1,0:T(8,128)(2,1)S(1)}, u32[]{:S(2)}, u32[]{:S(2)}) collective-permute-start(bf16[256,1024]{1,0:T(8,128)(2,1)S(1)} %broadcast_select_fusion.3), channel_id=1, source_target_pairs={{0,4},{4,0},{8,12},{12,8},{16,20},{20,16},{24,28},{28,24},{1,5},{5... | collective-permute-start | bytes 1572872 | tf_op jit(solution)/shard_map/ppermute | solution.py:475
  272.7 18.1 %collective-permute-start.23 = (bf16[256,1024]{1,0:T(8,128)(2,1)S(1)}, bf16[256,1024]{1,0:T(8,128)(2,1)S(1)}, u32[]{:S(2)}, u32[]{:S(2)}) collective-permute-start(bf16[256,1024]{1,0:T(8,128)(2,1)S(1)} %broadcast_select_fusion.2), channel_id=1, source_target_pairs={{0,4},{4,0},{8,12},{12,8},{16,20},{20,16},{24,28},{28,24},{1,5},{5... | collective-permute-start | bytes 1572872 | tf_op jit(solution)/shard_map/ppermute | solution.py:475
  273.0 29.7 %collective-permute-start.9 = (bf16[256,1024]{1,0:T(8,128)(2,1)S(1)}, bf16[256,1024]{1,0:T(8,128)(2,1)S(1)}, u32[]{:S(2)}, u32[]{:S(2)}) collective-permute-start(bf16[256,1024]{1,0:T(8,128)(2,1)S(1)} %add_convert_fusion.6), channel_id=1, source_target_pairs={{0,8},{8,0},{4,12},{12,4},{16,24},{24,16},{20,28},{28,20},{1,9},{9... | collective-permute-start | bytes 1572872 | tf_op jit(solution)/shard_map/ppermute | solution.py:469
  280.1 22.4 %collective-permute-start.20 = (bf16[256,1024]{1,0:T(8,128)(2,1)S(1)}, bf16[256,1024]{1,0:T(8,128)(2,1)S(1)}, u32[]{:S(2)}, u32[]{:S(2)}) collective-permute-start(bf16[256,1024]{1,0:T(8,128)(2,1)S(1)} %add_convert_fusion), channel_id=1, source_target_pairs={{0,8},{8,0},{4,12},{12,4},{16,24},{24,16},{20,28},{28,20},{1,9},{9... | collective-permute-start | bytes 1572872 | tf_op jit(solution)/shard_map/ppermute | solution.py:469
  (35 other events, 207.7 us)
Sparse Core Ops, SparseCore 0:
  9.9 46.7 all-gather.2
  58.5 43.9 all-gather.4
  128.5 54.6 all-reduce.3
  186.3 43.2 reduce-scatter.4
  232.7 43.9 reduce-scatter.2

commit v2 on v1

v2 whole, which is shorter than its diff:
```python
from functools import partial
import math

import jax
import jax.numpy as jnp
import numpy as np
from jax import lax
from jax.experimental import pallas as pl
from jax.experimental.pallas import tpu as pltpu
from jax.sharding import PartitionSpec as P

ROT = 16
UNIT = 128
EPS = 1e-05
F32 = jnp.float32
BF16 = jnp.bfloat16
VMEM_BYTES = 54 * 1024 * 1024

NN = (((1,), (0,)), ((), ()))
NT = (((1,), (1,)), ((), ()))
TN = (((0,), (0,)), ((), ()))


def mm(a, b, dims=NN):
    return lax.dot_general(a, b, dims, preferred_element_type=F32)


def split(a):
    hi = a.astype(BF16)
    return hi, (a - hi.astype(F32)).astype(BF16)


HELD_SPACE = pl.ANY
SMALL_COST = pl.CostEstimate(flops=1000, bytes_accessed=1000, transcendentals=0)


def params(grid_rank=1):
    return pltpu.CompilerParams(
        dimension_semantics=("arbitrary",) * grid_rank, vmem_limit_bytes=VMEM_BYTES
    )


def whole(shape):
    return pl.BlockSpec(shape, lambda *_: (0,) * len(shape))


def rows_of(block, width):
    return pl.BlockSpec((block, width), lambda i: (i, 0))


def norm_rows(x):
    mean = jnp.mean(x, axis=-1, keepdims=True)
    cent = x - mean
    inv = lax.rsqrt(jnp.mean(cent * cent, axis=-1, keepdims=True) + EPS)
    return cent * inv, inv


def chunk_place(units, pads, chunk, nseq):
    start = jnp.int32(0)
    pos, real, last = jnp.int32(0), jnp.int32(0), jnp.int32(0)
    for n in range(nseq):
        u = units[0, n]
        inside = (chunk >= start) & (chunk < start + u)
        pos = jnp.where(inside, chunk - start, pos)
        real = jnp.where(inside, (start + u - chunk) * UNIT - pads[0, n], real)
        last = jnp.where(inside, (chunk == start + u - 1).astype(jnp.int32), last)
        start = start + u
    return pos, real, last


def lanes(table, w):
    return jnp.concatenate([table] * (w // table.shape[1]), axis=1) if w > table.shape[1] else table


def turn(a, cosines, sines, low_half):
    w = a.shape[1]
    other = jnp.where(low_half, pltpu.roll(a, w - ROT // 2, 1), pltpu.roll(a, ROT // 2, 1))
    return a * cosines + other * sines


def head_stack(a, head_of_lane, heads):
    zero = jnp.zeros_like(a)
    return jnp.concatenate([jnp.where(head_of_lane == h, a, zero) for h in range(heads)], axis=0)


def side_by_side(a, heads):
    return jnp.concatenate([a[h * UNIT : (h + 1) * UNIT, :] for h in range(heads)], axis=1)


def masks(w, hd):
    lane = lax.broadcasted_iota(jnp.int32, (UNIT, w), 1)
    head_of_lane = lane // hd
    bi = lax.broadcasted_iota(jnp.int32, (w, w), 0) // hd
    bj = lax.broadcasted_iota(jnp.int32, (w, w), 1) // hd
    heads = w // hd
    row = lax.broadcasted_iota(jnp.int32, (heads * UNIT, UNIT), 0) % UNIT
    col = lax.broadcasted_iota(jnp.int32, (heads * UNIT, UNIT), 1)
    return head_of_lane, bi == bj, row >= col


def prep_kernel(hd, wqkv, bqkv, feat, pick, dct_bd, *refs):
    wqkv_o, bqkv_o, cf_o = refs[-3:]
    w = dct_bd.shape[0]
    wqkv_o[...] = mm(wqkv[...], pick[...]).astype(BF16)
    bqkv_o[...] = mm(jnp.broadcast_to(bqkv[...], (8, 3 * w)), pick[...])
    diag = lax.broadcasted_iota(jnp.int32, (w, w), 0) // hd == lax.broadcasted_iota(jnp.int32, (w, w), 1) // hd
    spread = jnp.where(diag, jnp.concatenate([feat[...].astype(F32)] * (w // hd), axis=1), 0.0)
    cf_hi, cf_lo = split(
        lax.dot_general(dct_bd[...], spread, NN, precision=lax.Precision.HIGHEST, preferred_element_type=F32)
    )
    cf_o[0] = cf_hi
    cf_o[1] = cf_lo


def prep_call(wqkv, bqkv, feat, pick, dct_bd, hd, deps=()):
    width, cols = wqkv.shape
    w = cols // 3
    sds = jax.ShapeDtypeStruct
    return pl.pallas_call(
        partial(prep_kernel, hd),
        in_specs=[whole(a.shape) for a in (wqkv, bqkv, feat, pick, dct_bd)] + unread(deps),
        out_shape=[sds((width, cols), BF16), sds((8, cols), F32), sds((2, w, w), BF16)],
        compiler_params=pltpu.CompilerParams(vmem_limit_bytes=VMEM_BYTES),
        cost_estimate=SMALL_COST,
        name="prepare",
    )(wqkv, bqkv, feat, pick, dct_bd, *deps)


def gelu_pair(h):
    bell = jnp.exp(h * h * -0.5)
    t = 1.0 / (1.0 + jnp.abs(h) * (0.3275911 * math.sqrt(0.5)))
    tail = bell * (
        t * (0.5 * 0.254829592 + t * (0.5 * -0.284496736 + t * (0.5 * 1.421413741 + t * (0.5 * -1.453152027 + t * (0.5 * 1.061405429)))))
    )
    cdf = jnp.where(h < 0.0, tail, 1.0 - tail)
    return h * cdf, cdf + (h * bell) * (1.0 / math.sqrt(2.0 * math.pi))


def pick_rows(refs, slot, into):
    if len(refs) == 1:
        return refs[0][...]
    rb = into.shape[0]
    for j, ref in enumerate(refs):
        at = slice(0, rb) if j < 3 else slice(0, rb // 2) if j == 3 else slice(rb // 2, rb)

        @pl.when(slot == min(j, 3))
        def _():
            into[at, :] = ref[...]

    return into[...]


def rows_specs(arrays, rb, at):
    if len(arrays) == 1:
        return [pl.BlockSpec((rb, arrays[0].shape[1]), at)]
    return [const(a.shape) for a in arrays]


def put(outs, slot, value):
    if len(outs) == 1:
        outs[0][...] = value
        return
    rb, half = value.shape[0], value.shape[1] // 2
    keep_a, send_a, keep_b, send_b = outs
    for j, (a, b) in enumerate(((keep_a, keep_b), (send_a, keep_b), (keep_a, send_b), (send_a, send_b))):

        @pl.when(slot == j)
        def _():
            a[(j // 2) * rb : (j // 2 + 1) * rb, :] = value[:, :half]
            b[(j % 2) * rb : (j % 2 + 1) * rb, :] = value[:, half:]


def put_specs(apart, rb, width, total, at):
    if apart:
        shape = (2 * rb, width // 2)
        return [whole(shape)] * 4, [jax.ShapeDtypeStruct(shape, BF16)] * 4
    return [pl.BlockSpec((rb, width), at)], [jax.ShapeDtypeStruct((total, width), BF16)]


def unread(arrays):
    return [pl.BlockSpec(memory_space=pl.ANY)] * len(arrays)


def const(shape):
    return pl.BlockSpec(shape, lambda *_: (0,) * len(shape), pipeline_mode=pl.Buffered(1))


def forward_kernel(hd, shards, nseq, meta, units, pads, *refs):
    x_refs = refs[:shards]
    vec, wqkv, bqkv, wfc_a, wfc_b, bfc_a, bfc_b, cf, cos_t, sin_t, wd, wp_a, wp_b = refs[shards : shards + 13]
    lna_o, lnm_o, act_o, gp_o, fq_o, fk_o, rq_o, rk_o, v_o, ao_o, o_o, rd_o, s_o, ks_o = refs[shards + 13 : shards + 27]
    *outs, xbuf, state, ksum = refs[shards + 27 :]
    step = pl.program_id(0)
    slot = meta[step]
    w, hh, per = v_o.shape[1], bfc_a.shape[1], xbuf.shape[0] // UNIT
    heads = w // hd

    @pl.when(step == 0)
    def _():
        state[...] = jnp.zeros_like(state)
        ksum[...] = jnp.zeros_like(ksum)

    xh, _ = norm_rows(pick_rows(x_refs, slot, xbuf).astype(F32))
    lna = (xh * vec[0:1, :] + vec[1:2, :]).astype(BF16)
    lnm = (xh * vec[2:3, :] + vec[3:4, :]).astype(BF16)
    lna_o[...] = lna
    lnm_o[...] = lnm
    qkv = mm(lna, wqkv[...]) + bqkv[0:1, :]
    v_o[...] = qkv[:, 2 * w :].astype(BF16)
    for cols, wfc, bfc in ((slice(0, hh), wfc_a, bfc_a), (slice(hh, 2 * hh), wfc_b, bfc_b)):
        act, slope = gelu_pair(mm(lnm, wfc[...]) + bfc[...])
        act_o[:, cols] = act.astype(BF16)
        gp_o[:, cols] = slope.astype(BF16)

    head_of_lane, diag, causal = masks(w, hd)
    low_half = lax.broadcasted_iota(jnp.int32, (UNIT, w), 1) % hd < ROT // 2
    row_id = lax.broadcasted_iota(jnp.int32, (UNIT, 1), 0)
    ones_bd = jnp.where(diag, 1.0, 0.0).astype(BF16)
    head_ones = head_stack(jnp.ones((UNIT, w), BF16), head_of_lane, heads)
    cf_hi, cf_lo = cf[0], cf[1]
    for i in range(per):
        pos, real, _ = chunk_place(units, pads, step * per + i, nseq)
        at = pl.ds(pl.multiple_of(pos * UNIT, UNIT), UNIT)
        cosines = lanes(cos_t[at, :], w)
        sines = lanes(sin_t[at, :], w)
        rows = slice(i * UNIT, (i + 1) * UNIT)
        rq = turn(qkv[rows, 0:w], cosines, sines, low_half)
        rk = turn(qkv[rows, w : 2 * w], cosines, sines, low_half)
        qh, ql = split(rq)
        kh, kl = split(rk)
        rq_o[rows, :] = qh
        rk_o[rows, :] = kh
        fq = jnp.exp(mm(qh, cf_hi) + mm(ql, cf_hi) + mm(qh, cf_lo)).astype(BF16)
        ek = jnp.exp(mm(kh, cf_hi) + mm(kl, cf_hi) + mm(kh, cf_lo))
        fk = jnp.where(row_id < real, ek, 0.0).astype(BF16)
        fq_o[rows, :] = fq
        fk_o[rows, :] = fk
        v = v_o[rows, :]
        keep = jnp.where(pos == 0, 0.0, 1.0)
        s_old = state[...] * keep
        k_old = ksum[...] * keep
        s_hi, s_lo = split(s_old)
        s_o[i, 0] = s_hi
        s_o[i, 1] = s_lo
        ks_o[i] = k_old
        scores = jnp.where(causal, mm(head_stack(fq, head_of_lane, heads), fk, NT), 0.0).astype(BF16)
        wide = side_by_side(scores, heads)
        num = mm(wide, head_stack(v, head_of_lane, heads)) + mm(fq, s_hi) + mm(fq, s_lo)
        p_hi, p_lo = split(fq.astype(F32) * k_old)
        den = mm(wide, head_ones) + mm(p_hi, ones_bd) + mm(p_lo, ones_bd)
        rden = 1.0 / den
        o = num * rden
        o_o[rows, :] = o
        rd_o[rows, :] = rden
        ao_o[rows, :] = o.astype(BF16)
        state[...] = s_old + jnp.where(diag, mm(fk, v, TN), 0.0)
        ksum[...] = k_old + jnp.sum(fk.astype(F32), axis=0, keepdims=True)

    out = mm(ao_o[...], wd[...]) + mm(act_o[:, :hh], wp_a[...]) + mm(act_o[:, hh:], wp_b[...])
    put(outs, slot, out.astype(BF16))


def forward_call(meta, units, pads, xs, vec, wqkv, bqkv, wfc, bfc, cf, cos_t, sin_t, wd, wp, hd, parts, rows):
    width, cols = wqkv.shape
    w, hid = cols // 3, wfc.shape[1]
    hh = hid // 2
    rb = rows // parts
    per, n = rb // UNIT, rows // UNIT
    core = meta.shape[0] - 1
    smem = pl.BlockSpec(memory_space=pltpu.SMEM)
    sds = jax.ShapeDtypeStruct

    def at(i, m):
        return (m[i], 0)

    def half(shape, index):
        return pl.BlockSpec(shape, index, pipeline_mode=pl.Buffered(1))

    out_specs, out_shape = put_specs(len(xs) > 1, rb, width, rows, at)
    saved = [(width, BF16)] * 2 + [(hid, BF16)] * 2 + [(w, BF16)] * 6 + [(w, F32)] * 2
    return pl.pallas_call(
        partial(forward_kernel, hd, len(xs), units.shape[1]),
        grid_spec=pltpu.PrefetchScalarGridSpec(
            num_scalar_prefetch=1,
            grid=(parts,),
            in_specs=[smem, smem]
            + rows_specs(xs, rb, at)
            + [
                const(vec.shape),
                const(wqkv.shape),
                const(bqkv.shape),
                half((width, hh), lambda i, m: (0, m[core])),
                half((width, hh), lambda i, m: (0, 1 - m[core])),
                half((1, hh), lambda i, m: (0, m[core])),
                half((1, hh), lambda i, m: (0, 1 - m[core])),
                const(cf.shape),
                const(cos_t.shape),
                const(sin_t.shape),
                const(wd.shape),
                half((hh, width), lambda i, m: (m[core], 0)),
                half((hh, width), lambda i, m: (1 - m[core], 0)),
            ],
            out_specs=[pl.BlockSpec((rb, k), at) for k, _ in saved]
            + [
                pl.BlockSpec((per, 2, w, w), lambda i, m: (m[i], 0, 0, 0)),
                pl.BlockSpec((per, 1, w), lambda i, m: (m[i], 0, 0)),
            ]
            + out_specs,
            scratch_shapes=[pltpu.VMEM((rb, width), BF16), pltpu.VMEM((w, w), F32), pltpu.VMEM((1, w), F32)],
        ),
        out_shape=[sds((rows, k), t) for k, t in saved] + [sds((n, 2, w, w), BF16), sds((n, 1, w), F32)] + out_shape,
        compiler_params=params(),
        cost_estimate=SMALL_COST,
        name="forward",
    )(meta, units, pads, *xs, vec, wqkv, bqkv, wfc, wfc, bfc, bfc, cf, cos_t, sin_t, wd, wp, wp)


def grad_kernel(meta, g_ref, gp, wd, wp_a, wp_b, *refs):
    dao_o, dh_o, sum_o, g_sum_o = refs[-4:]

    @pl.when(pl.program_id(0) == 0)
    def _():
        sum_o[...] = jnp.zeros_like(sum_o)
        g_sum_o[...] = jnp.zeros_like(g_sum_o)

    hh = wp_a.shape[0]
    g = g_ref[...]
    g_sum_o[...] += jnp.sum(g.astype(F32), axis=0, keepdims=True)
    dao_o[...] = mm(g, wd[...], NT).astype(BF16)
    for cols, wp in ((slice(0, hh), wp_a), (slice(hh, 2 * hh), wp_b)):
        dh = (mm(g, wp[...], NT) * gp[:, cols].astype(F32)).astype(BF16)
        dh_o[:, cols] = dh
        sum_o[:, cols] += jnp.sum(dh.astype(F32), axis=0, keepdims=True)


def grad_call(meta, parts, g, gp, wd, wp, deps=()):
    rows, hid = gp.shape
    w, width = wd.shape
    rb = rows // parts
    core = meta.shape[0] - 1
    sds = jax.ShapeDtypeStruct

    def plain(n):
        return pl.BlockSpec((rb, n), lambda i, m: (i, 0))

    return pl.pallas_call(
        grad_kernel,
        grid_spec=pltpu.PrefetchScalarGridSpec(
            num_scalar_prefetch=1,
            grid=(parts,),
            in_specs=[
                plain(width),
                plain(hid),
                const(wd.shape),
                pl.BlockSpec((hid // 2, width), lambda i, m: (m[core], 0), pipeline_mode=pl.Buffered(1)),
                pl.BlockSpec((hid // 2, width), lambda i, m: (1 - m[core], 0), pipeline_mode=pl.Buffered(1)),
            ]
            + unread(deps),
            out_specs=[plain(w), plain(hid), whole((1, hid)), whole((1, width))],
        ),
        out_shape=[sds((rows, w), BF16), sds((rows, hid), BF16), sds((1, hid), F32), sds((1, width), F32)],
        compiler_params=params(),
        cost_estimate=SMALL_COST,
        name="branch_grads",
    )(meta, g, gp, wd, wp, wp, *deps)


def attn_bwd_kernel(
    hd, nseq, meta, units, pads, dao, v_ref, o_ref, rd_ref, fq_ref, fk_ref, rq_ref, rk_ref, s_ref, ks_ref,
    cf, cos_t, sin_t, dct_bd, *refs,
):
    dqkv_o, sum_o, feat_o, after, after_sum, feat = refs[-6:]
    w = v_ref.shape[1]
    heads = w // hd
    step = pl.program_id(0)
    block = pl.num_programs(0) - 1 - step
    per = dao.shape[0] // UNIT

    @pl.when(step == 0)
    def _():
        for ref in (after, after_sum, feat, sum_o):
            ref[...] = jnp.zeros_like(ref)

    head_of_lane, diag, causal = masks(w, hd)
    low_half = lax.broadcasted_iota(jnp.int32, (UNIT, w), 1) % hd < ROT // 2
    ones_bd = jnp.where(diag, 1.0, 0.0).astype(BF16)
    cf_hi, cf_lo = cf[0], cf[1]
    for i in reversed(range(per)):
        pos, _, last = chunk_place(units, pads, block * per + i, nseq)
        rows = slice(i * UNIT, (i + 1) * UNIT)
        at = pl.ds(pl.multiple_of(pos * UNIT, UNIT), UNIT)
        cosines = lanes(cos_t[at, :], w)
        sines = -lanes(sin_t[at, :], w)
        keep = jnp.where(last == 1, 0.0, 1.0)
        a_old = after[...] * keep
        as_old = after_sum[...] * keep
        fq, fk, v = fq_ref[rows, :], fk_ref[rows, :], v_ref[rows, :]
        fqf, fkf = fq.astype(F32), fk.astype(F32)
        dn = (dao[rows, :].astype(F32) * rd_ref[rows, :]).astype(BF16)
        p_hi, p_lo = split(dn.astype(F32) * o_ref[rows, :])
        dden = -(mm(p_hi, ones_bd) + mm(p_lo, ones_bd))
        dn_s = head_stack(dn, head_of_lane, heads)
        fq_s = head_stack(fq, head_of_lane, heads)
        dden_s = jnp.concatenate(
            [jnp.broadcast_to(dden[:, h * hd : h * hd + 1], (UNIT, UNIT)) for h in range(heads)], axis=0
        )
        da = jnp.where(causal, mm(dn_s, v, NT) + dden_s, 0.0).astype(BF16)
        a = jnp.where(causal, mm(fq_s, fk, NT), 0.0).astype(BF16)
        s_hi, s_lo = s_ref[i, 0], s_ref[i, 1]
        dfq = (
            mm(side_by_side(da, heads), head_stack(fk, head_of_lane, heads))
            + mm(dn, s_hi, NT)
            + mm(dn, s_lo, NT)
            + dden * ks_ref[i]
        )
        a_hi, a_lo = split(a_old)
        dfk = mm(da, fq_s, TN) + mm(v, a_hi, NT) + mm(v, a_lo, NT) + as_old
        dv = mm(a, dn_s, TN) + mm(fk, a_hi) + mm(fk, a_lo)
        after[...] = a_old + jnp.where(diag, mm(fq, dn, TN), 0.0)
        after_sum[...] = as_old + jnp.sum(fqf * dden, axis=0, keepdims=True)
        dsq = (dfq * fqf).astype(BF16)
        dsk = (dfk * fkf).astype(BF16)
        feat[...] += mm(rq_ref[rows, :], dsq, TN) + mm(rk_ref[rows, :], dsk, TN)
        dq = turn(mm(dsq, cf_hi, NT) + mm(dsq, cf_lo, NT), cosines, sines, low_half)
        dk = turn(mm(dsk, cf_hi, NT) + mm(dsk, cf_lo, NT), cosines, sines, low_half)
        for j, part in enumerate((dq, dk, dv)):
            part = part.astype(BF16)
            dqkv_o[rows, j * w : (j + 1) * w] = part
            sum_o[:, j * w : (j + 1) * w] += jnp.sum(part.astype(F32), axis=0, keepdims=True)

    @pl.when(block == 0)
    def _():
        turned = lax.dot_general(
            dct_bd[...],
            jnp.where(diag, feat[...], 0.0),
            TN,
            precision=lax.Precision.HIGHEST,
            preferred_element_type=F32,
        )
        total = turned[0:hd, :]
        for h in range(1, heads):
            total = total + turned[h * hd : (h + 1) * hd, :]
        feat_o[...] = total


def attn_bwd_call(meta, units, pads, dao, v, o, rd, fq, fk, rq, rk, s, ks, cf, cos_t, sin_t, dct_bd, hd, parts, deps=()):
    rows, w = v.shape
    rb = rows // parts
    per = rb // UNIT
    smem = pl.BlockSpec(memory_space=pltpu.SMEM)
    sds = jax.ShapeDtypeStruct

    def at(i, m):
        return (m[parts - 1 - i], 0)

    return pl.pallas_call(
        partial(attn_bwd_kernel, hd, units.shape[1]),
        grid_spec=pltpu.PrefetchScalarGridSpec(
            num_scalar_prefetch=1,
            grid=(parts,),
            in_specs=[smem, smem]
            + [pl.BlockSpec((rb, w), at)] * 8
            + [
                pl.BlockSpec((per, 2, w, w), lambda i, m: (m[parts - 1 - i], 0, 0, 0)),
                pl.BlockSpec((per, 1, w), lambda i, m: (m[parts - 1 - i], 0, 0)),
                const(cf.shape),
                const(cos_t.shape),
                const(sin_t.shape),
                const(dct_bd.shape),
            ]
            + unread(deps),
            out_specs=[pl.BlockSpec((rb, 3 * w), at), whole((1, 3 * w)), whole((hd, w))],
            scratch_shapes=[pltpu.VMEM((w, w), F32), pltpu.VMEM((1, w), F32), pltpu.VMEM((w, w), F32)],
        ),
        out_shape=[sds((rows, 3 * w), BF16), sds((1, 3 * w), F32), sds((hd, w), F32)],
        compiler_params=params(),
        cost_estimate=SMALL_COST,
        name="attn_bwd",
    )(meta, units, pads, dao, v, o, rd, fq, fk, rq, rk, s, ks, cf, cos_t, sin_t, dct_bd, *deps)


SMALL_ROWS = 32


def norms_kernel(shards, deps, meta, *refs):
    x_refs = refs[:shards]
    dqkv, dh, vec, wqkv, wfc_a, wfc_b, g_sum, hid_sum, qkv_sum, feat, *rest = refs[shards:]
    small_o, *outs, xbuf = rest[deps:]
    step = pl.program_id(0)
    hh = wfc_a.shape[1]
    slot = step

    @pl.when(step == 0)
    def _():
        small_o[...] = jnp.zeros_like(small_o)
        hid_row = hid_sum[...]
        swapped = jnp.concatenate([hid_row[:, hh:], hid_row[:, :hh]], axis=1)
        hid_row = jnp.where(meta[meta.shape[0] - 1] == 1, swapped, hid_row)
        for at, row in ((4, g_sum[...]), (5, hid_row), (6, qkv_sum[...])):
            small_o[at : at + 1, 0 : row.shape[1]] = row
        deep, w = feat.shape
        each = deep * w // small_o.shape[1]
        for j in range(deep // each):
            small_o[8 : 8 + each, j * w : (j + 1) * w] = feat[j * each : (j + 1) * each, :]

    xh, _ = norm_rows(pick_rows(x_refs, slot, xbuf).astype(F32))
    da = mm(dqkv[...], wqkv[...], NT)
    small_o[0:1, :] += jnp.sum(da * xh, axis=0, keepdims=True)
    small_o[1:2, :] += jnp.sum(da, axis=0, keepdims=True)
    dm = mm(dh[:, :hh], wfc_a[...], NT) + mm(dh[:, hh:], wfc_b[...], NT)
    small_o[2:3, :] += jnp.sum(dm * xh, axis=0, keepdims=True)
    small_o[3:4, :] += jnp.sum(dm, axis=0, keepdims=True)
    put(outs, slot, (da * vec[0:1, :] + dm * vec[2:3, :]).astype(BF16))


def norms_call(meta, parts, xs, dqkv, dh, vec, wqkv, wfc, g_sum, hid_sum, qkv_sum, feat, deps=()):
    rows, hid = dh.shape
    width, cols = wqkv.shape
    hh = hid // 2
    rb = rows // parts
    core = meta.shape[0] - 1

    def at(i, m):
        return (i, 0)

    def to(i, m):
        return (m[i], 0)

    def half(shape, index):
        return pl.BlockSpec(shape, index, pipeline_mode=pl.Buffered(1))

    out_specs, out_shape = put_specs(len(xs) > 1, rb, width, rows, at)
    small = (SMALL_ROWS, width)
    return pl.pallas_call(
        partial(norms_kernel, len(xs), len(deps)),
        grid_spec=pltpu.PrefetchScalarGridSpec(
            num_scalar_prefetch=1,
            grid=(parts,),
            in_specs=rows_specs(xs, rb, at)
            + [
                pl.BlockSpec((rb, cols), at),
                pl.BlockSpec((rb, hid), at),
                const(vec.shape),
                const(wqkv.shape),
                half((width, hh), lambda i, m: (0, m[core])),
                half((width, hh), lambda i, m: (0, 1 - m[core])),
                const(g_sum.shape),
                const(hid_sum.shape),
                const(qkv_sum.shape),
                const(feat.shape),
            ]
            + unread(deps),
            out_specs=[whole(small)] + out_specs,
            scratch_shapes=[pltpu.VMEM((rb, width), BF16)],
        ),
        out_shape=[jax.ShapeDtypeStruct(small, F32)] + out_shape,
        compiler_params=params(),
        cost_estimate=SMALL_COST,
        name="norm_grads",
    )(meta, *xs, dqkv, dh, vec, wqkv, wfc, wfc, g_sum, hid_sum, qkv_sum, feat, *deps)


class Order:
    def __init__(self):
        self.last = None

    def after(self, *arrays):
        if self.last is None:
            return arrays if len(arrays) > 1 else arrays[0]
        self.last, *arrays = lax.optimization_barrier((self.last, *arrays))
        return tuple(arrays) if len(arrays) > 1 else arrays[0]

    def did(self, array):
        self.last = array
        return array


def both(a, b):
    return (a.astype(F32) + b.astype(F32)).astype(a.dtype)


def totals_kernel(count, mid, *refs):
    total = refs[-1]
    rows = refs[0].shape[0]
    for k in range(count):
        own, sent = refs[2 * k], refs[2 * k + 1]

        @pl.when(mid[0] == 1)
        def _():
            total[k * rows : (k + 1) * rows, :] = own[...]

        @pl.when(mid[0] == 0)
        def _():
            total[k * rows : (k + 1) * rows, :] = sent[...]


def totals_call(mid, pairs, deps):
    rows, cols = pairs[0].shape
    count = len(pairs) // 2
    return pl.pallas_call(
        partial(totals_kernel, count),
        in_specs=[pl.BlockSpec(memory_space=pltpu.SMEM)] + [whole((rows, cols))] * len(pairs) + unread(deps),
        out_specs=whole((count * rows, cols)),
        out_shape=jax.ShapeDtypeStruct((count * rows, cols), BF16),
        compiler_params=pltpu.CompilerParams(vmem_limit_bytes=VMEM_BYTES),
        cost_estimate=SMALL_COST,
        name="totals",
    )(mid.astype(jnp.int32).reshape(1), *pairs, *deps)


class Line:
    swap = [(i, i ^ 1) for i in range(8)]
    inward = [(0, 2), (1, 3), (6, 4), (7, 5)]
    inner = [(2, 4), (4, 2), (3, 5), (5, 3)]
    outward = [(2, 0), (3, 1), (4, 6), (5, 7)]

    def __init__(self, order):
        index = lax.axis_index("batch")
        self.order = order
        self.core, z = index % 2, index // 2
        self.mid = (z == 1) | (z == 2)
        self.own, self.sent = {}, {}

    def start(self, k, own, other):
        self.own[k], self.sent[k] = own, lax.ppermute(other, "batch", self.swap)

    def add(self, k, to):
        own, sent = self.order.after(self.own[k], self.sent[k])
        self.own[k] = self.order.did(both(own, sent))
        self.sent[k] = lax.ppermute(self.own[k], "batch", to)

    def go_in(self, k):
        self.add(k, self.inward)

    def meet(self, k):
        self.add(k, self.inner)

    def go_out(self, k):
        self.add(k, self.outward)

    def held(self, *ks):
        return tuple(self.own[k] for k in ks)

    def arrived(self, *ks):
        return tuple(self.sent[k] for k in ks)

    def landed(self, *ks):
        for k in ks:
            self.own[k], self.sent[k] = self.order.after(self.own[k], self.sent[k])

    def end(self, *ks, deps=()):
        self.landed(*ks)
        if deps:
            total = totals_call(self.mid, [a for k in ks for a in (self.own[k], self.sent[k])], deps)
        else:
            total = jnp.concatenate([jnp.where(self.mid, self.own[k], self.sent[k]) for k in ks])
        total = self.order.did(total)
        return total, lax.ppermute(total, "batch", self.swap)

    def end_small(self, k):
        self.landed(k)
        return jnp.where(self.mid, self.own[k], self.sent[k])


def across(a, mask):
    return lax.ppermute(a, "tensor", [(i, i ^ mask) for i in range(4)])


def part_of_batch(a):
    return lax.psum_scatter(a, "batch", scatter_dimension=0, tiled=True)


class TwoStepSum:
    def __init__(self, order, blocks):
        self.order = order
        self.keep_a, send_a, self.keep_b, send_b = blocks
        self.got_a, self.got_b = across(send_a, 1), across(send_b, 2)

    def second(self):
        rb = self.keep_a.shape[0] // 2
        self.got_a, self.got_b = self.order.after(self.got_a, self.got_b)
        a = both(self.keep_a[rb:], self.got_a[rb:])
        b = both(self.keep_b[rb:], self.got_b[rb:])
        a, b = lax.optimization_barrier((a, b))
        self.order.did(b)
        self.last_a, self.last_b = across(a, 2), across(b, 1)

    def result(self):
        rb = self.keep_a.shape[0] // 2
        terms = ((self.keep_a, self.got_a, self.last_a), (self.keep_b, self.got_b, self.last_b))
        return jnp.concatenate([sum(t[:rb].astype(F32) for t in side) for side in terms], axis=1)


def cosine_blocks(hd, heads):
    spatial = np.arange(hd, dtype=np.float64)[:, None]
    frequency = np.arange(hd, dtype=np.float64)[None, :]
    table = np.cos(math.pi * (2.0 * spatial + 1.0) * frequency / (2.0 * hd)) * math.sqrt(2.0 / hd)
    table[:, 0] *= math.sqrt(0.5)
    return np.kron(np.eye(heads), table).astype(np.float32)


def turn_tables(rows, hd):
    half = ROT // 2
    inverse_freq = np.exp(-math.log(10000.0) * 2.0 * np.arange(half) / ROT)
    angles = np.arange(rows)[:, None] * inverse_freq[None, :]
    cosines, sines = np.cos(angles), np.sin(angles)
    rest = np.ones((rows, hd - ROT))
    reps = (1, 128 // hd)
    return (
        np.tile(np.concatenate([cosines, cosines, rest], axis=1), reps).astype(np.float32),
        np.tile(np.concatenate([-sines, sines, 0.0 * rest], axis=1), reps).astype(np.float32),
    )


def column_pick(heads, hd):
    n = 3 * heads * hd
    source = np.arange(n).reshape(heads, 3, hd).transpose(1, 0, 2).reshape(-1)
    pick = np.zeros((n, n), np.float32)
    pick[source, np.arange(n)] = 1.0
    return pick


def body(
    tokens,
    output_grad,
    attn_norm_gain,
    attn_norm_bias,
    mlp_norm_gain,
    mlp_norm_bias,
    qkv_weight,
    qkv_bias,
    dense_weight,
    dense_bias,
    fc_weight,
    fc_bias,
    proj_weight,
    feature_weight,
    seq_units,
    pad_tokens,
):
    rows_dev, width = tokens.shape
    parts = lax.axis_size("tensor")
    n_batch = lax.axis_size("batch")
    rows = rows_dev * parts
    heads, hd, _ = feature_weight.shape
    w = heads * hd
    hid = fc_weight.shape[1]

    square = parts == 4 and n_batch == 8 and hid == width and 4 * w == width
    position = lax.axis_index("tensor")
    order = Order()
    line = Line(order) if square else None
    slots = jnp.arange(parts, dtype=jnp.int32)
    core = jnp.int32(0)
    if square:
        slots = slots ^ position
        core = line.core
        mid = rows_dev // 2
        a1, a2 = across(tokens, 1), across(tokens, 2)
    tail = jnp.stack([jnp.int32(rows_dev // UNIT), core.astype(jnp.int32)])
    meta = jnp.concatenate([slots, tail])
    vec = jnp.stack([attn_norm_gain, attn_norm_bias, mlp_norm_gain, mlp_norm_bias]).astype(F32)
    dct_bd = jnp.asarray(cosine_blocks(hd, heads))
    cos_t, sin_t = (jnp.asarray(t) for t in turn_tables(rows, hd))
    pick = jnp.asarray(column_pick(heads, hd)).astype(BF16)
    bfc = fc_bias.astype(F32).reshape(1, hid)
    wqkv, bqkv, cf_pair = prep_call(
        qkv_weight, qkv_bias.reshape(1, 3 * w), feature_weight.reshape(w, hd), pick, dct_bd, hd, (meta, vec, bfc)
    )
    hh = hid // 2
    dm = width // 2
    g_float = output_grad.astype(F32)
    x_own = tokens.astype(F32)
    if square:
        order.did(wqkv)
        a1, a2 = order.after(a1, a2)
        b1, b2 = across(a1[:mid], 2), across(a2[mid:], 1)
        b1, b2 = order.after(b1, b2)
        g_own, b1, b2 = lax.optimization_barrier((output_grad, b1, b2))
        c1, c2, c3 = across(g_own, 1), across(g_own, 2), across(g_own, 3)
        xs = [tokens, a1, a2, b1, b2]
    else:
        xs = [lax.all_gather(tokens, "tensor", axis=0, tiled=True)]
        g_all = lax.all_gather(output_grad, "tensor", axis=0, tiled=True)
    lna, lnm, act, gp, fq, fk, rq, rk, v, ao, o, rd, s, ks, *outs = forward_call(
        meta, seq_units, pad_tokens, xs, vec, wqkv, bqkv, fc_weight, bfc, cf_pair, cos_t, sin_t,
        dense_weight, proj_weight, hd, parts, rows,
    )
    order.did(ao)
    def residual(total):
        return (x_own + total + dense_bias.astype(F32)).astype(BF16)

    def proj_piece(k, cols):
        g = order.after(g_all)[:, cols]
        line.start(k, mm(act[:, :hh], g, TN).astype(BF16), order.did(mm(act[:, hh:], g, TN).astype(BF16)))

    def fc_piece(k, cols):
        part = order.after(lnm)[:, cols]
        line.start(k, mm(part, dh[:, :hh], TN).astype(BF16), order.did(mm(part, dh[:, hh:], TN).astype(BF16)))

    def rest_piece(k, cols):
        part, cotangent = order.after(lna, dqkv)
        stack = jnp.concatenate([mm(ao, g_all[:, cols], TN), mm(cotangent, part[:, cols], TN)])
        stack = stack.astype(BF16).reshape(2, 2 * w, dm)
        own = lax.dynamic_index_in_dim(stack, line.core, 0, keepdims=False)
        other = lax.dynamic_index_in_dim(stack, 1 - line.core, 0, keepdims=False)
        order.did(other)
        line.start(k, own, other)

    left, right = slice(0, dm), slice(dm, width)
    if square:
        branch = TwoStepSum(order, outs)
        c1, c2, c3 = order.after(c1, c2, c3)
        g_all = order.did(jnp.concatenate([output_grad, c1, c2, c3]))
        proj_piece(0, left)
        proj_piece(1, right)
        line.go_in(0)
        line.go_in(1)
        g_all = order.after(g_all)
    dao, dh, hid_sum, g_sum = grad_call(meta, parts, g_all, gp, dense_weight, proj_weight, line.held(0, 1) if square else ())
    order.did(dao)
    if square:
        branch.second()
        line.meet(0)
        fc_piece(2, left)
        line.go_in(2)
        fc_piece(3, right)
        line.meet(1)
        branch.last_a, branch.last_b = order.after(branch.last_a, branch.last_b)
        output = order.did(residual(branch.result()))
        line.go_out(0)
        line.go_in(3)
    dao = order.after(dao)
    dqkv, qkv_sum, feat = attn_bwd_call(
        meta, seq_units, pad_tokens, dao, v, o, rd, fq, fk, rq, rk, s, ks, cf_pair, cos_t, sin_t, dct_bd, hd, parts,
        (*line.held(0, 1, 2, 3), output) if square else (),
    )
    order.did(dqkv)
    if square:
        line.meet(2)
        line.go_out(1)
        rest_piece(4, left)
        line.landed(0)
        line.meet(3)
        line.go_in(4)
        rest_piece(5, right)
        line.go_in(5)
        line.landed(1)
        line.go_out(2)
    dqkv = order.after(dqkv)
    small, *es = norms_call(meta, parts, xs, dqkv, dh, vec, wqkv, fc_weight, g_sum, hid_sum, qkv_sum, feat,
        (*line.held(2, 3, 4, 5), *line.arrived(0, 1)) if square else ())
    order.did(small)

    def rows_grad(e):
        x_hat, inv_std = norm_rows(x_own)
        mean = jnp.mean(e, axis=-1, keepdims=True)
        return (g_float + inv_std * (e - mean - x_hat * jnp.mean(e * x_hat, axis=-1, keepdims=True))).astype(BF16)

    if square:
        line.meet(4)
        line.go_out(3)
        line.landed(2)
        small = order.after(small)
        line.start(6, small, small)
        es[1], es[3] = order.after(es[1], es[3])
        e_sum = TwoStepSum(order, es)
        line.go_in(6)
        line.meet(5)
        line.landed(3)
        first = line.end(0, 1, 2, 3)
        line.meet(6)
        line.go_out(4)
        second = line.core == 1

        def pieces_of(pair, count):
            own, twin = order.after(*pair)
            low = jnp.where(second, twin, own).reshape(count, 2 * w, dm)
            high = jnp.where(second, own, twin).reshape(count, 2 * w, dm)
            return low, high

        low, high = pieces_of(first, 4)
        proj_grad = order.did(
            jnp.concatenate(
                [jnp.concatenate([low[k], high[k]], axis=0) for k in (0, 1)], axis=1
            ).astype(F32)
        )
        e_sum.second()
        line.go_out(6)
        fc_grad = order.did(
            jnp.concatenate([jnp.concatenate([low[k], high[k]], axis=1) for k in (2, 3)], axis=0).astype(F32)
        )
        line.go_out(5)
        small = order.did(line.end_small(6))
        norm_sums = small[:8]
        hop = across(norm_sums, 1)
        e_sum.last_a, e_sum.last_b = order.after(e_sum.last_a, e_sum.last_b)
        tokens_grad = order.did(rows_grad(e_sum.result()))
        norm_sums = order.did(norm_sums + order.after(hop))
        hop = across(norm_sums, 2)
        last = line.end(4, 5, deps=(proj_grad, fc_grad, tokens_grad, norm_sums))
        norm_sums = norm_sums + order.after(hop)
        low, high = pieces_of(last, 2)
        rest = jnp.concatenate([jnp.concatenate([low[k], high[k]], axis=0) for k in (0, 1)], axis=1)
        dense_grad, qkv_grad = rest[:w].astype(F32), rest[w:]
        hid_sum = small[5]
        pick = jnp.asarray(column_pick(heads, hd)).astype(BF16)
        qkv_grad = lax.dot_general(qkv_grad.astype(BF16), pick, (((0,), (1,)), ((), ())), preferred_element_type=F32)
    else:
        output = residual(lax.psum_scatter(outs[0], "tensor", scatter_dimension=0, tiled=True).astype(F32))
        tokens_grad = rows_grad(lax.psum_scatter(es[0], "tensor", scatter_dimension=0, tiled=True).astype(F32))
        sums = [mm(act, g_all, TN), mm(lnm, dh, TN), mm(ao, g_all, TN), mm(dqkv, lna, TN)]
        sums = lax.psum([a.astype(BF16) for a in sums], "batch")
        proj_grad, fc_grad, dense_grad, qkv_grad = (a.astype(F32) for a in sums)
        small = lax.psum(small, "batch")
        norm_sums = lax.psum(small[:4], "tensor")
        hid_sum = small[5, :hid]
        qkv_grad = qkv_grad.reshape(3, heads, hd, width).transpose(3, 1, 0, 2).reshape(width, 3 * w)
    each = hd * w // width
    feature_grad = small[8 : 8 + each].reshape(each, width // w, heads, hd).transpose(2, 1, 0, 3).reshape(heads, hd, hd)
    qkv_bias_grad = small[6, : 3 * w].reshape(3, heads, hd).transpose(1, 0, 2).reshape(3 * w)

    return (
        output,
        tokens_grad,
        norm_sums[0],
        norm_sums[1],
        norm_sums[2],
        norm_sums[3],
        qkv_grad,
        qkv_bias_grad,
        dense_grad,
        small[4],
        fc_grad,
        hid_sum,
        proj_grad,
        feature_grad,
    )


def solution(mesh):
    rows = P(("batch", "tensor"), None)
    placed = (
        rows,
        rows,
        P(),
        P(),
        P(),
        P(),
        P(None, "tensor"),
        P("tensor"),
        P("tensor", None),
        P(),
        P(None, "tensor"),
        P("tensor"),
        P("tensor", None),
        P("tensor", None, None),
        P("batch", None),
        P("batch", None),
    )
    return jax.shard_map(
        body,
        mesh=mesh,
        in_specs=placed,
        out_specs=(
            rows,
            rows,
            P(),
            P(),
            P(),
            P(),
            P(None, "tensor"),
            P("tensor"),
            P("tensor", None),
            P(),
            P(None, "tensor"),
            P("tensor"),
            P("tensor", None),
            P("tensor", None, None),
        ),
        check_vma=False,
    )
```

time: 367 us -> 272 us (0.74)
  blocking collectives: 61.1 us -> 0 us
  waiting for transfers between devices: 92.7 us -> 46.4 us
  starting transfers between devices: 48.7 us -> 75.1 us
  between operations: 14.7 us -> 2.26 us
  local copies, waits for them, and re-layouts: 24.6 us -> 14.4 us
  Pallas kernels: 71.2 us -> 81 us
  other arithmetic: 35.9 us -> 30.6 us
    psum x2 -> x0, blocking collectives: 61.1 us -> none  [the longest x1 39.9 us: body(): lax.psum((norm_sums, jnp.sum(g_own, axis=0)), ('batch', 'tensor'))]
    all_gather x2 -> x0, waiting for transfers between devices: 54.9 us -> none  [the longest x1 35.1 us: body(): x_all = lax.all_gather(tokens, 'tensor', axis=0, tiled=True)]
    ppermute x26 -> x47, starting transfers between devices: 48.3 us -> 75.1 us  [the longest x21 50.9 us: add(): self.sent[k] = lax.ppermute(self.own[k], 'batch', to)]
    ppermute x26 -> x47, waiting for transfers between devices: 36.3 us -> 46.4 us  [the longest x21 23.4 us: add(): self.sent[k] = lax.ppermute(self.own[k], 'batch', to)]
    pallas_call x6, Pallas kernels: 71.2 us -> 81 us  [the longest x1 33.9 us: forward_call(): pl.pallas_call(partial(forward_kernel, hd, len(xs), units.shape[1]), grid...]
    select_n x10 -> x7, other arithmetic: 11.2 us -> 3.75 us  [the longest x2 3.5 us: pieces_of(): low = jnp.where(second, twin, own).reshape(count, 2 * w, dm)]
    convert_element_type x17 -> x27, other arithmetic: 15 us -> 20.5 us  [the longest x22 12.6 us: both(): return (a.astype(F32) + b.astype(F32)).astype(a.dtype)]
    unnamed x57 -> x89, local copies, waits for them, and re-layouts: 10.2 us -> 5.78 us
  transfers between devices with their start and end apart: 31 -> 47, of which waited for: 6 -> 12; matrix products, arithmetic and copies ran while one was open for 19% -> 20% of each run, Pallas kernels for 13% -> 29%
where the time goes in v2:
time: 272 us; the launch traced here: 268 us
  Pallas kernels  81 us (30%)
  starting transfers between devices  75.1 us (28%)
  waiting for transfers between devices  46.4 us (17%)
  other arithmetic  30.6 us (11%)
  matrix products  18.3 us (7%)
  local copies, waits for them, and re-layouts  14.4 us (5%)
    ppermute x21, starting transfers between devices, add(): self.sent[k] = lax.ppermute(self.own[k], 'batch', to)  50.9 us
    pallas_call x1, Pallas kernels, forward_call(): pl.pallas_call(partial(forward_kernel, hd, len(xs), units.shape[1]), grid...  33.9 us
    ppermute x21, waiting for transfers between devices, add(): self.sent[k] = lax.ppermute(self.own[k], 'batch', to)  23.4 us
    ppermute x17, starting transfers between devices, across(): return lax.ppermute(a, 'tensor', [(i, i ^ mask) for i in range(4)])  22.7 us
    ppermute x17, waiting for transfers between devices, across(): return lax.ppermute(a, 'tensor', [(i, i ^ mask) for i in range(4)])  21.8 us
    pallas_call x1, Pallas kernels, attn_bwd_call(): pl.pallas_call(partial(attn_bwd_kernel, hd, units.shape[1]), grid_spec=pl...  15.9 us
    dot_general x12, matrix products, mm(): return lax.dot_general(a, b, dims, preferred_element_type=F32)  15.2 us
    pallas_call x1, Pallas kernels, norms_call(): pl.pallas_call(partial(norms_kernel, len(xs), len(deps)), grid_spec=pltpu...  13.9 us
  transfers between devices with their start and end apart: 47, of which 12 were waited for; matrix products, arithmetic and copies ran while one was open for 20% of the time, Pallas kernels for 29%

profile of v2, /device:TPU:0, one launch (start us, length us, event | category | flops | bytes accessed | tf_op | source)
XLA Modules:
  0.0 268.0 jit_solution(1006263091547550087)
XLA Ops:
  0.6 3.0 %collective-permute-start = (bf16[384,1024]{1,0:T(8,128)(2,1)}, bf16[384,1024]{1,0:T(8,128)(2,1)S(1)}, u32[]{:S(2)}, u32[]{:S(2)}) collective-permute-start(bf16[384,1024]{1,0:T(8,128)(2,1)} %refs_0_.3), channel_id=1, source_target_pairs={{0,1},{1,0},{2,3},{3,2},{4,5},{5,4},{6,7},{7,6},{8,9},{9,8},{10,11... | collective-permute-start | bytes 2359304 | tf_op jit(solution)/shard_map/ppermute | solution.py:666
  11.7 4.9 %prepare.1 = (bf16[1024,768]{1,0:T(8,128)(2,1)}, f32[8,768]{1,0:T(8,128)}, bf16[2,256,256]{2,1,0:T(8,128)(2,1)}) custom-call(bf16[1024,768]{1,0:T(8,128)(2,1)} %wqkv.1, bf16[1,768]{1,0:T(2,128)(2,1)} %reshape.111.bqkv, bf16[256,64]{1,0:T(8,128)(2,1)} %bitcast.34, bf16[768,768]{1,0:T(8,128)(2,1)} %constant.72.pick, f32[256,256]{1,0:T(8,128)} %constant.66.clone.dct_bd, ...), custom_call_target="tpu_custom_call" | custom-call | flops 1000 | bytes 1000 | tf_op jit(solution)/shard_map/prepare/pallas_call | solution.py:119
  16.6 4.8 %collective-permute-done.refs_1_ = bf16[384,1024]{1,0:T(8,128)(2,1)S(1)} collective-permute-done((bf16[384,1024]{1,0:T(8,128)(2,1)}, bf16[384,1024]{1,0:T(8,128)(2,1)S(1)}, u32[]{:S(2)}, u32[]{:S(2)}) %collective-permute-start) | collective-permute-done | bytes 786464 | tf_op jit(solution)/shard_map/ppermute | solution.py:666
  25.1 7.5 %collective-permute-done.2.refs_3_ = bf16[192,1024]{1,0:T(8,128)(2,1)S(1)} collective-permute-done((bf16[192,1024]{1,0:T(8,128)(2,1)S(1)}, bf16[192,1024]{1,0:T(8,128)(2,1)S(1)}, u32[]{:S(2)}, u32[]{:S(2)}) %collective-permute-start.2) | collective-permute-done | bytes 393248 | tf_op jit(solution)/shard_map/ppermute | solution.py:666
  37.7 33.9 %forward.1 = (bf16[1536,1024]{1,0:T(8,128)(2,1)}, bf16[1536,1024]{1,0:T(8,128)(2,1)}, bf16[1536,1024]{1,0:T(8,128)(2,1)}, bf16[1536,1024]{1,0:T(8,128)(2,1)}, bf...) custom-call(s32[6]{0:T(128)} %pad_add_fusion.refs_0_.meta, ...), custom_call_target="tpu_custom_call" | custom-call | flops 1000 | bytes 1000 | tf_op jit(solution)/shard_map/forward/pallas_call | solution.py:281
  81.8 3.5 %collective-permute-start.11 = (bf16[512,512]{1,0:T(8,128)(2,1)S(1)}, bf16[512,512]{1,0:T(8,128)(2,1)S(1)}, u32[]{:S(2)}, u32[]{:S(2)}) collective-permute-start(bf16[512,512]{1,0:T(8,128)(2,1)S(1)} %add_convert_fusion.17.refs_0_), channel_id=1, source_target_pairs={{0,8},{4,12},{24,16},{28,20},{1,9},{5,13},{25,17},{29,21},{2,10},{... | collective-permute-start | bytes 1572872 | tf_op jit(solution)/shard_map/ppermute | solution.py:630
  86.8 9.8 %branch_grads.1 = (bf16[1536,256]{1,0:T(8,128)(2,1)}, bf16[1536,1024]{1,0:T(8,128)(2,1)}, f32[1,1024]{1,0:T(1,128)}, f32[1,1024]{1,0:T(1,128)}) custom-call(s32[6]{0:T(128)} %pad_add_fusion.refs_0_.meta, bf16[1536,1024]{1,0:T(8,128)(2,1)} %copy-done.5, bf16[1536,1024]{1,0:T(8,128)(2,1)} %get-tuple-element.175.gp, bf16[256,1024]{1,0:T(8,128)(2,1)} %wd.1, ...), custom_call_target="tpu_custom_call" | custom-call | flops 1000 | bytes 1000 | tf_op jit(solution)/shard_map/branch_grads/pallas_call | solution.py:346
  99.9 2.6 fusion.72
  105.9 5.1 %collective-permute-start.18 = (bf16[512,512]{1,0:T(8,128)(2,1)}, bf16[512,512]{1,0:T(8,128)(2,1)S(1)}, u32[]{:S(2)}, u32[]{:S(2)}) collective-permute-start(bf16[512,512]{1,0:T(8,128)(2,1)} %add_convert_fusion.14.refs_2_), channel_id=1, source_target_pairs={{0,8},{4,12},{24,16},{28,20},{1,9},{5,13},{25,17},{29,21},{2,10},{... | collective-permute-start | bytes 1572872 | tf_op jit(solution)/shard_map/ppermute | solution.py:630
  118.1 6.6 %collective-permute-start.20 = (bf16[512,512]{1,0:T(8,128)(2,1)S(1)}, bf16[512,512]{1,0:T(8,128)(2,1)S(1)}, u32[]{:S(2)}, u32[]{:S(2)}) collective-permute-start(bf16[512,512]{1,0:T(8,128)(2,1)S(1)} %add_convert_fusion.11.refs_3_), channel_id=1, source_target_pairs={{0,8},{4,12},{24,16},{28,20},{1,9},{5,13},{25,17},{29,21},{2,10},{... | collective-permute-start | bytes 1572872 | tf_op jit(solution)/shard_map/ppermute | solution.py:630
  124.7 15.9 %attn_bwd.1 = (bf16[1536,768]{1,0:T(8,128)(2,1)}, f32[1,768]{1,0:T(1,128)}, f32[64,256]{1,0:T(8,128)}) custom-call(s32[6]{0:T(128)} %pad_add_fusion.refs_0_.meta, s32[1,4]{1,0:T(1,128)} %units.3, s32[1,4]{1,0:T(1,128)} %pads.3, bf16[1536,256]{1,0:T(8,128)(2,1)} %get-tuple-element.200.dao, bf16[1536,256]{1,0:T(8,128)(2,1)} %get-tuple-element.201.v_ref, ...), custom_call_target="tpu_custom_call" | custom-call | flops 1000 | bytes 1000 | tf_op jit(solution)/shard_map/attn_bwd/pallas_call | solution.py:456
  143.3 2.8 %fusion.22 = bf16[768,512]{1,0:T(8,128)(2,1)S(1)} fusion(bf16[1536,768]{1,0:T(8,128)(2,1)S(1)} %copy-done.21, bf16[1536,1024]{1,0:T(8,128)(2,1)} %get-tuple-element.230), kind=kOutput, calls=%fused_computation.32 | convolution fusion | flops 1208352768 | bytes 4718592 | tf_op jit(solution)/shard_map/dot_general | solution.py:25
  153.9 7.4 %collective-permute-start.26 = (bf16[512,512]{1,0:T(8,128)(2,1)}, bf16[512,512]{1,0:T(8,128)(2,1)S(1)}, u32[]{:S(2)}, u32[]{:S(2)}) collective-permute-start(bf16[512,512]{1,0:T(8,128)(2,1)} %add_convert_fusion.6.refs_17_), channel_id=1, source_target_pairs={{0,8},{4,12},{24,16},{28,20},{1,9},{5,13},{25,17},{29,21},{2,10},{... | collective-permute-start | bytes 1572872 | tf_op jit(solution)/shard_map/ppermute | solution.py:630
  163.7 8.0 %collective-permute-start.30 = (bf16[512,512]{1,0:T(8,128)(2,1)S(1)}, bf16[512,512]{1,0:T(8,128)(2,1)S(1)}, u32[]{:S(2)}, u32[]{:S(2)}) collective-permute-start(bf16[512,512]{1,0:T(8,128)(2,1)S(1)} %add_convert_fusion.5.refs_18_), channel_id=1, source_target_pairs={{0,8},{4,12},{24,16},{28,20},{1,9},{5,13},{25,17},{29,21},{2,10},{... | collective-permute-start | bytes 1572872 | tf_op jit(solution)/shard_map/ppermute | solution.py:630
  172.5 13.9 %norm_grads.1 = (f32[32,1024]{1,0:T(8,128)}, bf16[768,512]{1,0:T(8,128)(2,1)}, bf16[768,512]{1,0:T(8,128)(2,1)}, bf16[768,512]{1,0:T(8,128)(2,1)}, bf16[768,512]{1,0:T(8,128)(2,1)}) custom-call(s32[6]{0:T(128)} %pad_add_fusion.refs_0_.meta, bf16[384,1024]{1,0:T(8,128)(2,1)} %refs_0_.3, bf16[384,1024]{1,0:T(8,128)(2,1)} %copy-done.3, ...), custom_call_target="tpu_custom_call" | custom-call | flops 1000 | bytes 1000 | tf_op jit(solution)/shard_map/norm_grads/pallas_call | solution.py:534
  192.8 11.2 %collective-permute-done.31 = bf16[512,512]{1,0:T(8,128)(2,1)S(1)} collective-permute-done((bf16[512,512]{1,0:T(8,128)(2,1)S(1)}, bf16[512,512]{1,0:T(8,128)(2,1)S(1)}, u32[]{:S(2)}, u32[]{:S(2)}) %collective-permute-start.31) | collective-permute-done | bytes 524320 | tf_op jit(solution)/shard_map/ppermute | solution.py:630
  205.8 3.5 %collective-permute-start.32 = (f32[32,1024]{1,0:T(8,128)S(1)}, f32[32,1024]{1,0:T(8,128)S(1)}, u32[]{:S(2)}, u32[]{:S(2)}) collective-permute-start(f32[32,1024]{1,0:T(8,128)S(1)} %add.174), channel_id=1, source_target_pairs={{0,8},{4,12},{24,16},{28,20},{1,9},{5,13},{25,17},{29,21},{2,10},{... | collective-permute-start | bytes 393224 | tf_op jit(solution)/shard_map/ppermute | solution.py:630
  218.9 2.6 maximum_convert_fusion.1.refs_5_
  221.5 2.6 maximum_convert_fusion.refs_4_
  224.1 4.9 %collective-permute-done.35 = bf16[768,512]{1,0:T(8,128)(2,1)S(1)} collective-permute-done((bf16[768,512]{1,0:T(8,128)(2,1)}, bf16[768,512]{1,0:T(8,128)(2,1)S(1)}, u32[]{:S(2)}, u32[]{:S(2)}) %collective-permute-start.35) | collective-permute-done | bytes 786464 | tf_op jit(solution)/shard_map/ppermute | solution.py:666
  235.3 6.3 %collective-permute-done.39 = f32[32,1024]{1,0:T(8,128)S(1)} collective-permute-done((f32[32,1024]{1,0:T(8,128)S(1)}, f32[32,1024]{1,0:T(8,128)S(1)}, u32[]{:S(2)}, u32[]{:S(2)}) %collective-permute-start.39) | collective-permute-done | bytes 131104 | tf_op jit(solution)/shard_map/ppermute | solution.py:630
  246.4 5.6 %collective-permute-done.44.refs_3_ = bf16[512,512]{1,0:T(8,128)(2,1)S(1)} collective-permute-done((bf16[512,512]{1,0:T(8,128)(2,1)S(1)}, bf16[512,512]{1,0:T(8,128)(2,1)S(1)}, u32[]{:S(2)}, u32[]{:S(2)}) %collective-permute-start.44) | collective-permute-done | bytes 524320 | tf_op jit(solution)/shard_map/ppermute | solution.py:630
  252.8 2.6 totals.1
  264.4 3.1 %fusion.12 = f32[1024,768]{1,0:T(8,128)} fusion(bf16[768,768]{1,0:T(8,128)(2,1)S(1)} %copy-done.29, bf16[1024,1024]{1,0:T(8,128)(2,1)S(1)} %maximum_maximum_fusion), kind=kOutput, calls=%fused_computation.21 | convolution fusion | flops 1207959552 | bytes 5898240 | tf_op jit(solution)/shard_map/dot_general | solution.py:908
  (259 shorter events, 93.6 us)
Async XLA Ops:
  0.6 20.8 %collective-permute-start = (bf16[384,1024]{1,0:T(8,128)(2,1)}, bf16[384,1024]{1,0:T(8,128)(2,1)S(1)}, u32[]{:S(2)}, u32[]{:S(2)}) collective-permute-start(bf16[384,1024]{1,0:T(8,128)(2,1)} %refs_0_.3), channel_id=1, source_target_pairs={{0,1},{1,0},{2,3},{3,2},{4,5},{5,4},{6,7},{7,6},{8,9},{9,8},{10,11... | collective-permute-start | bytes 2359304 | tf_op jit(solution)/shard_map/ppermute | solution.py:666
  3.6 19.2 %collective-permute-start.1 = (bf16[384,1024]{1,0:T(8,128)(2,1)}, bf16[384,1024]{1,0:T(8,128)(2,1)S(1)}, u32[]{:S(2)}, u32[]{:S(2)}) collective-permute-start(bf16[384,1024]{1,0:T(8,128)(2,1)} %refs_0_.3), channel_id=1, source_target_pairs={{0,2},{1,3},{2,0},{3,1},{4,6},{5,7},{6,4},{7,5},{8,10},{9,11},{10,... | collective-permute-start | bytes 2359304 | tf_op jit(solution)/shard_map/ppermute | solution.py:666
  34.0 39.1 %collective-permute-start.4 = (bf16[384,1024]{1,0:T(8,128)(2,1)S(1)}, bf16[384,1024]{1,0:T(8,128)(2,1)}, u32[]{:S(2)}, u32[]{:S(2)}) collective-permute-start(bf16[384,1024]{1,0:T(8,128)(2,1)S(1)} %copy-done.19), channel_id=1, source_target_pairs={{0,1},{1,0},{2,3},{3,2},{4,5},{5,4},{6,7},{7,6},{8,9},{9,8},{10,11... | collective-permute-start | bytes 2359304 | tf_op jit(solution)/shard_map/ppermute | solution.py:666
  34.8 38.3 %collective-permute-start.5 = (bf16[384,1024]{1,0:T(8,128)(2,1)S(1)}, bf16[384,1024]{1,0:T(8,128)(2,1)}, u32[]{:S(2)}, u32[]{:S(2)}) collective-permute-start(bf16[384,1024]{1,0:T(8,128)(2,1)S(1)} %copy-done.19), channel_id=1, source_target_pairs={{0,2},{1,3},{2,0},{3,1},{4,6},{5,7},{6,4},{7,5},{8,10},{9,11},{10,... | collective-permute-start | bytes 2359304 | tf_op jit(solution)/shard_map/ppermute | solution.py:666
  35.3 37.8 %collective-permute-start.6 = (bf16[384,1024]{1,0:T(8,128)(2,1)S(1)}, bf16[384,1024]{1,0:T(8,128)(2,1)}, u32[]{:S(2)}, u32[]{:S(2)}) collective-permute-start(bf16[384,1024]{1,0:T(8,128)(2,1)S(1)} %copy-done.19), channel_id=1, source_target_pairs={{0,3},{1,2},{2,1},{3,0},{4,7},{5,6},{6,5},{7,4},{8,11},{9,10},{10,... | collective-permute-start | bytes 2359304 | tf_op jit(solution)/shard_map/ppermute | solution.py:666
  71.7 25.0 %collective-permute-start.10 = (bf16[768,512]{1,0:T(8,128)(2,1)}, bf16[768,512]{1,0:T(8,128)(2,1)S(1)}, u32[]{:S(2)}, u32[]{:S(2)}) collective-permute-start(bf16[768,512]{1,0:T(8,128)(2,1)} %get-tuple-element.178), channel_id=1, source_target_pairs={{0,2},{1,3},{2,0},{3,1},{4,6},{5,7},{6,4},{7,5},{8,10},{9,11},{10,... | collective-permute-start | bytes 2359304 | tf_op jit(solution)/shard_map/ppermute | solution.py:666
  72.2 24.5 %collective-permute-start.9 = (bf16[768,512]{1,0:T(8,128)(2,1)}, bf16[768,512]{1,0:T(8,128)(2,1)S(1)}, u32[]{:S(2)}, u32[]{:S(2)}) collective-permute-start(bf16[768,512]{1,0:T(8,128)(2,1)} %get-tuple-element.177), channel_id=1, source_target_pairs={{0,1},{1,0},{2,3},{3,2},{4,5},{5,4},{6,7},{7,6},{8,9},{9,8},{10,11... | collective-permute-start | bytes 2359304 | tf_op jit(solution)/shard_map/ppermute | solution.py:666
  81.8 18.0 %collective-permute-start.11 = (bf16[512,512]{1,0:T(8,128)(2,1)S(1)}, bf16[512,512]{1,0:T(8,128)(2,1)S(1)}, u32[]{:S(2)}, u32[]{:S(2)}) collective-permute-start(bf16[512,512]{1,0:T(8,128)(2,1)S(1)} %add_convert_fusion.17.refs_0_), channel_id=1, source_target_pairs={{0,8},{4,12},{24,16},{28,20},{1,9},{5,13},{25,17},{29,21},{2,10},{... | collective-permute-start | bytes 1572872 | tf_op jit(solution)/shard_map/ppermute | solution.py:630
  85.5 26.6 %collective-permute-start.13 = (bf16[512,512]{1,0:T(8,128)(2,1)S(1)}, bf16[512,512]{1,0:T(8,128)(2,1)S(1)}, u32[]{:S(2)}, u32[]{:S(2)}) collective-permute-start(bf16[512,512]{1,0:T(8,128)(2,1)S(1)} %add_convert_fusion.16.refs_1_), channel_id=1, source_target_pairs={{0,8},{4,12},{24,16},{28,20},{1,9},{5,13},{25,17},{29,21},{2,10},{... | collective-permute-start | bytes 1572872 | tf_op jit(solution)/shard_map/ppermute | solution.py:630
  96.9 16.2 %collective-permute-start.14 = (bf16[384,512]{1,0:T(8,128)(2,1)S(1)}, bf16[384,512]{1,0:T(8,128)(2,1)S(1)}, u32[]{:S(2)}, u32[]{:S(2)}) collective-permute-start(bf16[384,512]{1,0:T(8,128)(2,1)S(1)} %add_convert_fusion.21), channel_id=1, source_target_pairs={{0,2},{1,3},{2,0},{3,1},{4,6},{5,7},{6,4},{7,5},{8,10},{9,11},{10,... | collective-permute-start | bytes 1179656 | tf_op jit(solution)/shard_map/ppermute | solution.py:666
  105.9 34.7 %collective-permute-start.18 = (bf16[512,512]{1,0:T(8,128)(2,1)}, bf16[512,512]{1,0:T(8,128)(2,1)S(1)}, u32[]{:S(2)}, u32[]{:S(2)}) collective-permute-start(bf16[512,512]{1,0:T(8,128)(2,1)} %add_convert_fusion.14.refs_2_), channel_id=1, source_target_pairs={{0,8},{4,12},{24,16},{28,20},{1,9},{5,13},{25,17},{29,21},{2,10},{... | collective-permute-start | bytes 1572872 | tf_op jit(solution)/shard_map/ppermute | solution.py:630
  113.1 28.9 %collective-permute-start.21 = (bf16[512,512]{1,0:T(8,128)(2,1)}, bf16[512,512]{1,0:T(8,128)(2,1)S(1)}, u32[]{:S(2)}, u32[]{:S(2)}) collective-permute-start(bf16[512,512]{1,0:T(8,128)(2,1)} %add_convert_fusion.13.refs_1_), channel_id=1, source_target_pairs={{8,16},{16,8},{12,20},{20,12},{9,17},{17,9},{13,21},{21,13},{10,18... | collective-permute-start | bytes 1572872 | tf_op jit(solution)/shard_map/ppermute | solution.py:630
  115.6 33.8 %collective-permute-start.24 = (bf16[512,512]{1,0:T(8,128)(2,1)S(1)}, bf16[512,512]{1,0:T(8,128)(2,1)S(1)}, u32[]{:S(2)}, u32[]{:S(2)}) collective-permute-start(bf16[512,512]{1,0:T(8,128)(2,1)S(1)} %add_convert_fusion.12.refs_0_), channel_id=1, source_target_pairs={{8,0},{12,4},{16,24},{20,28},{9,1},{13,5},{17,25},{21,29},{10,2},{... | collective-permute-start | bytes 1572872 | tf_op jit(solution)/shard_map/ppermute | solution.py:630
  118.1 31.4 %collective-permute-start.20 = (bf16[512,512]{1,0:T(8,128)(2,1)S(1)}, bf16[512,512]{1,0:T(8,128)(2,1)S(1)}, u32[]{:S(2)}, u32[]{:S(2)}) collective-permute-start(bf16[512,512]{1,0:T(8,128)(2,1)S(1)} %add_convert_fusion.11.refs_3_), channel_id=1, source_target_pairs={{0,8},{4,12},{24,16},{28,20},{1,9},{5,13},{25,17},{29,21},{2,10},{... | collective-permute-start | bytes 1572872 | tf_op jit(solution)/shard_map/ppermute | solution.py:630
  147.0 24.7 %collective-permute-start.25 = (bf16[512,512]{1,0:T(8,128)(2,1)S(1)}, bf16[512,512]{1,0:T(8,128)(2,1)S(1)}, u32[]{:S(2)}, u32[]{:S(2)}) collective-permute-start(bf16[512,512]{1,0:T(8,128)(2,1)S(1)} %add_convert_fusion.7), channel_id=1, source_target_pairs={{8,0},{12,4},{16,24},{20,28},{9,1},{13,5},{17,25},{21,29},{10,2},{... | collective-permute-start | bytes 1572872 | tf_op jit(solution)/shard_map/ppermute | solution.py:630
  153.9 32.5 %collective-permute-start.26 = (bf16[512,512]{1,0:T(8,128)(2,1)}, bf16[512,512]{1,0:T(8,128)(2,1)S(1)}, u32[]{:S(2)}, u32[]{:S(2)}) collective-permute-start(bf16[512,512]{1,0:T(8,128)(2,1)} %add_convert_fusion.6.refs_17_), channel_id=1, source_target_pairs={{0,8},{4,12},{24,16},{28,20},{1,9},{5,13},{25,17},{29,21},{2,10},{... | collective-permute-start | bytes 1572872 | tf_op jit(solution)/shard_map/ppermute | solution.py:630
  161.3 27.2 %collective-permute-start.27 = (bf16[512,512]{1,0:T(8,128)(2,1)}, bf16[512,512]{1,0:T(8,128)(2,1)S(1)}, u32[]{:S(2)}, u32[]{:S(2)}) collective-permute-start(bf16[512,512]{1,0:T(8,128)(2,1)} %add_convert_fusion.8.refs_16_), channel_id=1, source_target_pairs={{8,16},{16,8},{12,20},{20,12},{9,17},{17,9},{13,21},{21,13},{10,18... | collective-permute-start | bytes 1572872 | tf_op jit(solution)/shard_map/ppermute | solution.py:630
  162.2 29.0 %collective-permute-start.28 = (bf16[512,512]{1,0:T(8,128)(2,1)S(1)}, bf16[512,512]{1,0:T(8,128)(2,1)S(1)}, u32[]{:S(2)}, u32[]{:S(2)}) collective-permute-start(bf16[512,512]{1,0:T(8,128)(2,1)S(1)} %add_convert_fusion.9.refs_15_), channel_id=1, source_target_pairs={{8,0},{12,4},{16,24},{20,28},{9,1},{13,5},{17,25},{21,29},{10,2},{... | collective-permute-start | bytes 1572872 | tf_op jit(solution)/shard_map/ppermute | solution.py:630
  163.7 29.0 %collective-permute-start.30 = (bf16[512,512]{1,0:T(8,128)(2,1)S(1)}, bf16[512,512]{1,0:T(8,128)(2,1)S(1)}, u32[]{:S(2)}, u32[]{:S(2)}) collective-permute-start(bf16[512,512]{1,0:T(8,128)(2,1)S(1)} %add_convert_fusion.5.refs_18_), channel_id=1, source_target_pairs={{0,8},{4,12},{24,16},{28,20},{1,9},{5,13},{25,17},{29,21},{2,10},{... | collective-permute-start | bytes 1572872 | tf_op jit(solution)/shard_map/ppermute | solution.py:630
  209.3 19.6 %collective-permute-start.35 = (bf16[768,512]{1,0:T(8,128)(2,1)}, bf16[768,512]{1,0:T(8,128)(2,1)S(1)}, u32[]{:S(2)}, u32[]{:S(2)}) collective-permute-start(bf16[768,512]{1,0:T(8,128)(2,1)} %get-tuple-element.267), channel_id=1, source_target_pairs={{0,1},{1,0},{2,3},{3,2},{4,5},{5,4},{6,7},{7,6},{8,9},{9,8},{10,11... | collective-permute-start | bytes 2359304 | tf_op jit(solution)/shard_map/ppermute | solution.py:666
  210.6 19.3 %collective-permute-start.36 = (bf16[768,512]{1,0:T(8,128)(2,1)}, bf16[768,512]{1,0:T(8,128)(2,1)S(1)}, u32[]{:S(2)}, u32[]{:S(2)}) collective-permute-start(bf16[768,512]{1,0:T(8,128)(2,1)} %get-tuple-element.268), channel_id=1, source_target_pairs={{0,2},{1,3},{2,0},{3,1},{4,6},{5,7},{6,4},{7,5},{8,10},{9,11},{10,... | collective-permute-start | bytes 2359304 | tf_op jit(solution)/shard_map/ppermute | solution.py:666
  213.1 17.9 %collective-permute-start.38 = (f32[32,1024]{1,0:T(8,128)S(1)}, f32[32,1024]{1,0:T(8,128)S(1)}, u32[]{:S(2)}, u32[]{:S(2)}) collective-permute-start(f32[32,1024]{1,0:T(8,128)S(1)} %add.176), channel_id=1, source_target_pairs={{8,16},{16,8},{12,20},{20,12},{9,17},{17,9},{13,21},{21,13},{10,18... | collective-permute-start | bytes 393224 | tf_op jit(solution)/shard_map/ppermute | solution.py:630
  215.1 31.3 %collective-permute-start.43 = (bf16[512,512]{1,0:T(8,128)(2,1)S(1)}, bf16[512,512]{1,0:T(8,128)(2,1)S(1)}, u32[]{:S(2)}, u32[]{:S(2)}) collective-permute-start(bf16[512,512]{1,0:T(8,128)(2,1)S(1)} %add_convert_fusion.1.refs_0_), channel_id=1, source_target_pairs={{8,0},{12,4},{16,24},{20,28},{9,1},{13,5},{17,25},{21,29},{10,2},{... | collective-permute-start | bytes 1572872 | tf_op jit(solution)/shard_map/ppermute | solution.py:630
  234.0 18.0 %collective-permute-start.44 = (bf16[512,512]{1,0:T(8,128)(2,1)S(1)}, bf16[512,512]{1,0:T(8,128)(2,1)S(1)}, u32[]{:S(2)}, u32[]{:S(2)}) collective-permute-start(bf16[512,512]{1,0:T(8,128)(2,1)S(1)} %add_convert_fusion.refs_2_), channel_id=1, source_target_pairs={{8,0},{12,4},{16,24},{20,28},{9,1},{13,5},{17,25},{21,29},{10,2},{... | collective-permute-start | bytes 1572872 | tf_op jit(solution)/shard_map/ppermute | solution.py:630
  (66 other events, 458.1 us)
